TPU v7x, 128 devices: a whole 4x4x4 slice. The times are simulated.
128 devices in a mesh: row: 16 (over y_lo, x, core), col: 8 (over z, y_hi).
Axes of the slice: x: 4, y: 4 (y_hi: 2, y_lo: 2; y = y_hi * 2 + y_lo), z: 4, core: 2. Of those that a mesh axis runs over, the one named last changes fastest.
Arguments:
- latent: bfloat16 [1, 128, 256, 640], P(None, 'row', 'col'), may hold values from -6 to 6
- timestep: int32 [1], replicated, may hold values from 0 to 499
- noise_seed: int32 [1], replicated, may hold values from 0 to 999999
- proj_seed: int32 [1], replicated, may hold values from 0 to 999999
- example_ids: int32 [1], replicated, may hold values from 0 to 99999
- time_weight: bfloat16 [640, 640], replicated, may hold values from -0.25 to 0.25
- conv1_weight: bfloat16 [5760, 640], replicated, may hold values from -0.078125 to 0.078125
- conv2_weight: bfloat16 [5760, 640], replicated, may hold values from -0.078125 to 0.078125
Outputs:
- section_out: bfloat16 [1, 128, 256, 640], P(None, 'row', 'col')
- sketch: float32 [1, 1024], replicated
All inputs are finite; a program needn't handle non-finite values.
Results may differ from a plain program's by a relative error of at most 0.013.
Values may be sent and summed in bfloat16 or wider, within the bound.
A program may use at most 128 MiB of HBM per device.

v0:
```python
import math

import jax
import jax.numpy as jnp
from jax import lax
from jax.sharding import PartitionSpec as P

K = 1024


def extended(cells, sides, width):
    for axis, dim in sides:
        count = lax.axis_size(axis)
        ends = count - 1
        head = lax.slice_in_dim(cells, 0, width, axis=dim)
        tail = lax.slice_in_dim(cells, cells.shape[dim] - width, cells.shape[dim], axis=dim)
        cells = jnp.concatenate(
            [
                lax.ppermute(tail, axis, [(i, (i + 1) % count) for i in range(ends)]),
                cells,
                lax.ppermute(head, axis, [((i + 1) % count, i) for i in range(ends)]),
            ],
            axis=dim,
        )
    return cells


def mix_bits(value):
    value = value ^ lax.shift_right_logical(value, jnp.int32(16))
    value = value * jnp.int32(2146121005)
    value = value ^ lax.shift_right_logical(value, jnp.int32(15))
    value = value * jnp.int32(-2073254261)
    value = value ^ lax.shift_right_logical(value, jnp.int32(16))
    return value


def noise_field(
    example_ids,
    noise_seed,
    row_first,
    col_first,
    tile_rows,
    tile_cols,
    channels,
    rows_all,
    cols_all,
):
    row_ids = row_first + jnp.arange(tile_rows, dtype=jnp.int32)
    col_ids = col_first + jnp.arange(tile_cols, dtype=jnp.int32)
    chan_ids = jnp.arange(channels, dtype=jnp.int32)
    base = (
        (example_ids[:, None, None, None] * rows_all + row_ids[None, :, None, None]) * cols_all
        + col_ids[None, None, :, None]
    ) * channels + chan_ids
    salt = mix_bits(noise_seed[0])
    total = jnp.zeros(base.shape, jnp.float32)
    for salt_index in range(4):
        bits = mix_bits(base * 4 + salt_index + salt)
        total = total + lax.shift_right_logical(bits, jnp.int32(8)).astype(jnp.float32) * (
            1.0 / 16777216.0
        )
    return (total - 2.0) * math.sqrt(3.0)


def plan(timestep):
    fraction = timestep.astype(jnp.float32) / 1000.0
    return jnp.cos((fraction + 0.008) / 1.008 * (math.pi / 2.0)) ** 2


def time_features(timestep, channels):
    half = channels // 2
    freqs = jnp.exp(-math.log(10000.0) * jnp.arange(half, dtype=jnp.float32) / half)
    angles = timestep.astype(jnp.float32)[:, None] * freqs[None, :]
    return jnp.concatenate([jnp.sin(angles), jnp.cos(angles)], axis=1)


def sign_block(first_index, width, proj_count, salt):
    flat_ids = first_index + jnp.arange(width, dtype=jnp.int32)
    column_ids = jnp.arange(proj_count, dtype=jnp.int32)
    bits = mix_bits(flat_ids[:, None] * proj_count + column_ids[None, :] + salt)
    return jnp.where(bits < 0, -1.0, 1.0).astype(jnp.float32)


def unfold(padded, tile_rows, tile_cols):
    pieces = []
    for row_off in range(3):
        for col_off in range(3):
            pieces.append(
                padded[:, row_off : row_off + tile_rows, col_off : col_off + tile_cols, :]
            )
    joined = jnp.concatenate(pieces, axis=3)
    return joined.reshape(joined.shape[0], tile_rows * tile_cols, joined.shape[3])


def on_device(
    latent, timestep, noise_seed, proj_seed, example_ids, time_weight, conv1_weight, conv2_weight
):
    batch, tile_rows, tile_cols, channels = latent.shape
    rows_count = lax.axis_size("row")
    cols_count = lax.axis_size("col")
    rows_all = tile_rows * rows_count
    cols_all = tile_cols * cols_count
    row_first = lax.axis_index("row") * tile_rows
    col_first = lax.axis_index("col") * tile_cols
    noise = noise_field(
        example_ids,
        noise_seed,
        row_first,
        col_first,
        tile_rows,
        tile_cols,
        channels,
        rows_all,
        cols_all,
    )
    abar = plan(timestep)[:, None, None, None]
    noisy = (jnp.sqrt(abar) * latent.astype(jnp.float32) + jnp.sqrt(1.0 - abar) * noise).astype(
        jnp.bfloat16
    )
    act = jax.nn.silu(noisy.astype(jnp.float32)).astype(jnp.bfloat16)
    act_pad = extended(act, (("row", 1), ("col", 2)), 1)
    features = time_features(timestep, channels).astype(jnp.bfloat16)
    temb = jnp.dot(features, time_weight, preferred_element_type=jnp.float32)
    act_cols = unfold(act_pad, tile_rows, tile_cols).reshape(
        batch * tile_rows * tile_cols, 9 * channels
    )
    pre = jnp.dot(act_cols, conv1_weight, preferred_element_type=jnp.float32).reshape(
        batch, tile_rows, tile_cols, channels
    )
    hidden = jax.nn.silu(pre + temb[:, None, None, :]).astype(jnp.bfloat16)
    hid_pad = extended(hidden, (("row", 1), ("col", 2)), 1)
    hid_cols = unfold(hid_pad, tile_rows, tile_cols)
    conv_out = jnp.dot(
        hid_cols.reshape(batch * tile_rows * tile_cols, 9 * channels),
        conv2_weight,
        preferred_element_type=jnp.float32,
    )
    out_full = noisy.astype(jnp.float32) + conv_out.reshape(batch, tile_rows, tile_cols, channels)
    section_out = out_full.astype(jnp.bfloat16)
    cot = ((out_full - noise) / math.sqrt(rows_all * cols_all)).astype(jnp.bfloat16)
    cot = cot.reshape(batch, tile_rows * tile_cols, channels)
    owned = channels // (rows_count * cols_count)
    value = jnp.einsum("bpo,bpq->obq", cot, hid_cols, preferred_element_type=jnp.float32)
    grad = lax.psum_scatter(
        value.reshape(lax.axis_size(("row", "col")) * owned, batch * 9 * channels),
        ("row", "col"),
        scatter_dimension=0,
        tiled=True,
    )
    chan_first = (lax.axis_index("row") * cols_count + lax.axis_index("col")) * owned
    grad = grad.reshape(owned, batch, 9 * channels)
    salt = mix_bits(proj_seed[0] + jnp.int32(12345))

    def accumulate(step, total):
        out_chan = chan_first + step
        block = sign_block(out_chan * (9 * channels), 9 * channels, K, salt)
        rows_now = lax.dynamic_slice_in_dim(grad, step, 1, 0)[0]
        return total + jnp.dot(
            rows_now, block, preferred_element_type=jnp.float32, precision=lax.Precision.HIGHEST
        )

    partial_sketch = lax.fori_loop(0, owned, accumulate, jnp.zeros((batch, K), jnp.float32))
    sketch = lax.psum(partial_sketch / math.sqrt(9.0 * channels * channels), ("row", "col"))
    return (section_out, sketch)


def solution(mesh):
    placed = (P(None, "row", "col", None), P(), P(), P(), P(), P(), P(), P())
    return jax.shard_map(
        on_device,
        mesh=mesh,
        in_specs=placed,
        out_specs=(P(None, "row", "col", None), P()),
        check_vma=False,
    )
```

profile of v0, /device:TPU:1, one launch (start us, length us, event | category | flops | bytes accessed | tf_op | source)
XLA Modules:
  0.0 444.1 jit_solution(15715743970670146007)
XLA Ops:
  9.5 2.4 fusion.73
  12.0 4.6 %collective-permute-start = (bf16[1,1,32,640]{3,2,1,0:T(8,128)(2,1)S(1)}, bf16[1,1,32,640]{3,2,1,0:T(8,128)(2,1)S(1)}, u32[]{:S(2)}, u32[]{:S(2)}) collective-permute-start(bf16[1,1,32,640]{3,2,1,0:T(8,128)(2,1)S(1)} %get-tuple-element.159), channel_id=1, source_target_pairs={{0,8},{8,16},{16,24},{24,32},{32,40},{40,48},{48,56},{56,64},{64,7... | collective-permute-start | bytes 122888 | tf_op jit(solution)/shard_map/ppermute | solution.py:19
  16.6 1.9 collective-permute-start.1
  18.7 3.2 collective-permute-done.1
  22.0 4.8 %collective-permute-start.2 = (bf16[1,10,1,640]{3,2,1,0:T(2,128)(2,1)S(1)}, bf16[1,10,1,640]{3,2,1,0:T(2,128)(2,1)S(1)}, u32[]{:S(2)}, u32[]{:S(2)}) collective-permute-start(bf16[1,10,1,640]{3,2,1,0:T(2,128)(2,1)S(1)} %get-tuple-element.156), channel_id=1, source_target_pairs={{0,1},{1,2},{2,3},{3,4},{4,5},{5,6},{6,7},{8,9},{9,10},{10,11},{11... | collective-permute-start | bytes 38408 | tf_op jit(solution)/shard_map/ppermute | solution.py:19
  28.4 4.5 %collective-permute-done.3 = bf16[1,10,1,640]{3,2,1,0:T(2,128)(2,1)S(1)} collective-permute-done((bf16[1,10,1,640]{3,2,1,0:T(2,128)(2,1)S(1)}, bf16[1,10,1,640]{3,2,1,0:T(2,128)(2,1)S(1)}, u32[]{:S(2)}, u32[]{:S(2)}) %collective-permute-start.3) | collective-permute-done | bytes 12832 | tf_op jit(solution)/shard_map/ppermute | solution.py:21
  36.0 2.5 multiply_convert_fusion.1
  38.5 3.3 collective-permute-start.4
  41.9 1.9 collective-permute-start.5
  43.8 3.4 collective-permute-done.5
  47.2 4.2 collective-permute-start.6
  53.0 4.5 %collective-permute-done.7 = bf16[1,10,1,640]{3,2,1,0:T(2,128)(2,1)S(1)} collective-permute-done((bf16[1,10,1,640]{3,2,1,0:T(2,128)(2,1)S(1)}, bf16[1,10,1,640]{3,2,1,0:T(2,128)(2,1)S(1)}, u32[]{:S(2)}, u32[]{:S(2)}) %collective-permute-start.7) | collective-permute-done | bytes 12832 | tf_op jit(solution)/shard_map/ppermute | solution.py:21
  61.1 4.4 multiply_convert_fusion
  65.5 7.7 %convolution_bitcast_fusion = f32[640,5760]{0,1:T(8,128)} fusion(bf16[256,640]{1,0:T(8,128)(2,1)S(1)} %bitcast.94, bf16[1,256,5760]{2,1,0:T(8,128)(2,1)S(1)} %constant_dynamic-update-slice_fusion.10), kind=kOutput, calls=%fused_computation.29 | convolution fusion | flops 1887436800 | bytes 18022400 | tf_op jit(solution)/shard_map/bpo,bpq->obq/dot_general | solution.py:143
  73.8 177.2 %all-reduce.3.cloned.1.call-done = f32[640,5760]{0,1:T(8,128)} async-done(((f32[640,5760]{0,1:T(8,128)}), f32[640,5760]{0,1:T(8,128)}) %all-reduce.3.cloned.1.call-update) | async-done | bytes 14745616
  251.0 5.1 %dynamic-slice_bitcast_fusion = f32[5,1,5760]{0,2,1:T(8,128)} fusion(f32[640,5760]{0,1:T(8,128)} %all-reduce.3.cloned.1.call-done, u32[]{:T(128)S(6)} %multiply.39), kind=kLoop, calls=%fused_computation.34 | loop fusion | bytes 230404 | tf_op jit(solution)/shard_map/reshape | solution.py:151
  256.1 2.4 copy.11
  258.5 114.8 %while.14 = (s32[]{:T(128)}, f32[1,1024]{1,0:T(1,128)S(1)}, f32[5,1,5760]{2,1,0:T(1,128)S(1)}, s32[]{:T(128)}, s32[]{:T(128)}, /*index=5*/s32[]{:T(128)}, s32[]{:T(128)}, s32[]{:T(128)}) while((s32[]{:T(128)}, f32[1,1024]{1,0:T(1,128)S(1)}, f32[5,1,5760]{2,1,0:T(1,128)S(1)}, s32[]{:T(128)}, s32[]{:T(128)}, /*index=5*/s32[]{:T(128)}, ...), condition=%wide.region_2.3_spmd.clone, body=%wide.region_1.2_spmd.clone.sunk | while | flops 141571328 | bytes 78979 | solution.py:162
  273.4 20.0 %fusion.92 = f32[1,1024]{1,0:T(1,128)S(1)} fusion(s32[]{:T(128)} %get-tuple-element.215, s32[5760]{0:T(1024)S(1)} %add_multiply_fusion.4, f32[5,1,5760]{2,1,0:T(1,128)S(1)} %get-tuple-element.213, s32[]{:T(128)} %get-tuple-element.203, f32[1,1024]{1,0:T(1,128)S(1)} %get-tuple-element.204, pred[]{:T(512)S(6)} %compare.3), kind=kOutput, calls=%fused_computation.17.clone.1 | convolution fusion | flops 141559808 | bytes 55817 | tf_op jit(solution)/shard_map/while/body/eval_jaxpr/dot_general | solution.py:158
  293.4 20.0 %fusion.92 = f32[1,1024]{1,0:T(1,128)S(1)} fusion(s32[]{:T(128)} %get-tuple-element.215, s32[5760]{0:T(1024)S(1)} %add_multiply_fusion.4, f32[5,1,5760]{2,1,0:T(1,128)S(1)} %get-tuple-element.213, s32[]{:T(128)} %get-tuple-element.203, f32[1,1024]{1,0:T(1,128)S(1)} %get-tuple-element.204, pred[]{:T(512)S(6)} %compare.3), kind=kOutput, calls=%fused_computation.17.clone.1 | convolution fusion | flops 141559808 | bytes 55817 | tf_op jit(solution)/shard_map/while/body/eval_jaxpr/dot_general | solution.py:158
  313.3 20.0 %fusion.92 = f32[1,1024]{1,0:T(1,128)S(1)} fusion(s32[]{:T(128)} %get-tuple-element.215, s32[5760]{0:T(1024)S(1)} %add_multiply_fusion.4, f32[5,1,5760]{2,1,0:T(1,128)S(1)} %get-tuple-element.213, s32[]{:T(128)} %get-tuple-element.203, f32[1,1024]{1,0:T(1,128)S(1)} %get-tuple-element.204, pred[]{:T(512)S(6)} %compare.3), kind=kOutput, calls=%fused_computation.17.clone.1 | convolution fusion | flops 141559808 | bytes 55817 | tf_op jit(solution)/shard_map/while/body/eval_jaxpr/dot_general | solution.py:158
  333.3 20.0 %fusion.92 = f32[1,1024]{1,0:T(1,128)S(1)} fusion(s32[]{:T(128)} %get-tuple-element.215, s32[5760]{0:T(1024)S(1)} %add_multiply_fusion.4, f32[5,1,5760]{2,1,0:T(1,128)S(1)} %get-tuple-element.213, s32[]{:T(128)} %get-tuple-element.203, f32[1,1024]{1,0:T(1,128)S(1)} %get-tuple-element.204, pred[]{:T(512)S(6)} %compare.3), kind=kOutput, calls=%fused_computation.17.clone.1 | convolution fusion | flops 141559808 | bytes 55817 | tf_op jit(solution)/shard_map/while/body/eval_jaxpr/dot_general | solution.py:158
  353.3 20.0 %fusion.92 = f32[1,1024]{1,0:T(1,128)S(1)} fusion(s32[]{:T(128)} %get-tuple-element.215, s32[5760]{0:T(1024)S(1)} %add_multiply_fusion.4, f32[5,1,5760]{2,1,0:T(1,128)S(1)} %get-tuple-element.213, s32[]{:T(128)} %get-tuple-element.203, f32[1,1024]{1,0:T(1,128)S(1)} %get-tuple-element.204, pred[]{:T(512)S(6)} %compare.3), kind=kOutput, calls=%fused_computation.17.clone.1 | convolution fusion | flops 141559808 | bytes 55817 | tf_op jit(solution)/shard_map/while/body/eval_jaxpr/dot_general | solution.py:158
  373.2 63.8 %psum.7 = f32[1,1024]{1,0:T(1,128)} all-reduce(f32[1,1024]{1,0:T(1,128)S(1)} %broadcast_multiply_fusion), channel_id=1, replica_groups=mesh['row'=16,'col'=8] {'row','col'}, use_global_device_ids=true, to_apply=%region_3.4 | all-reduce | flops 1024 | bytes 8192 | tf_op jit(solution)/shard_map/psum | solution.py:163
  (66 shorter events, 10.0 us)
Async XLA Ops:
  7.2 20.9 %copy-start = (bf16[640,640]{1,0:T(8,128)(2,1)S(1)}, bf16[640,640]{1,0:T(8,128)(2,1)}, u32[]{:S(2)}) copy-start(bf16[640,640]{1,0:T(8,128)(2,1)} %param.15) | copy-start | bytes 2457604
  7.2 243.9 %all-reduce.3.cloned.1.call-start = ((), (), s32[]{:S(2)}) async-start(), calls=%async_computation | async-start | bytes 29491200
  11.9 21.4 %copy-start.1 = (bf16[1,8,32,640]{3,2,1,0:T(8,128)(2,1)S(1)}, bf16[1,8,32,640]{3,2,1,0:T(8,128)(2,1)}, u32[]{:S(2)}) copy-start(bf16[1,8,32,640]{3,2,1,0:T(8,128)(2,1)} %param.10) | copy-start | bytes 983044
  12.0 6.7 %collective-permute-start = (bf16[1,1,32,640]{3,2,1,0:T(8,128)(2,1)S(1)}, bf16[1,1,32,640]{3,2,1,0:T(8,128)(2,1)S(1)}, u32[]{:S(2)}, u32[]{:S(2)}) collective-permute-start(bf16[1,1,32,640]{3,2,1,0:T(8,128)(2,1)S(1)} %get-tuple-element.159), channel_id=1, source_target_pairs={{0,8},{8,16},{16,24},{24,32},{32,40},{40,48},{48,56},{56,64},{64,7... | collective-permute-start | bytes 122888 | tf_op jit(solution)/shard_map/ppermute | solution.py:19
  16.6 5.3 %collective-permute-start.1 = (bf16[1,1,32,640]{3,2,1,0:T(8,128)(2,1)S(1)}, bf16[1,1,32,640]{3,2,1,0:T(8,128)(2,1)S(1)}, u32[]{:S(2)}, u32[]{:S(2)}) collective-permute-start(bf16[1,1,32,640]{3,2,1,0:T(8,128)(2,1)S(1)} %get-tuple-element.160), channel_id=1, source_target_pairs={{8,0},{16,8},{24,16},{32,24},{40,32},{48,40},{56,48},{64,56},{72,6... | collective-permute-start | bytes 122888 | tf_op jit(solution)/shard_map/ppermute | solution.py:21
  22.0 6.4 %collective-permute-start.2 = (bf16[1,10,1,640]{3,2,1,0:T(2,128)(2,1)S(1)}, bf16[1,10,1,640]{3,2,1,0:T(2,128)(2,1)S(1)}, u32[]{:S(2)}, u32[]{:S(2)}) collective-permute-start(bf16[1,10,1,640]{3,2,1,0:T(2,128)(2,1)S(1)} %get-tuple-element.156), channel_id=1, source_target_pairs={{0,1},{1,2},{2,3},{3,4},{4,5},{5,6},{6,7},{8,9},{9,10},{10,11},{11... | collective-permute-start | bytes 38408 | tf_op jit(solution)/shard_map/ppermute | solution.py:19
  26.8 6.1 %collective-permute-start.3 = (bf16[1,10,1,640]{3,2,1,0:T(2,128)(2,1)S(1)}, bf16[1,10,1,640]{3,2,1,0:T(2,128)(2,1)S(1)}, u32[]{:S(2)}, u32[]{:S(2)}) collective-permute-start(bf16[1,10,1,640]{3,2,1,0:T(2,128)(2,1)S(1)} %get-tuple-element.155), channel_id=1, source_target_pairs={{1,0},{2,1},{3,2},{4,3},{5,4},{6,5},{7,6},{9,8},{10,9},{11,10},{12... | collective-permute-start | bytes 38408 | tf_op jit(solution)/shard_map/ppermute | solution.py:21
  32.9 3.1 copy-start.2
  38.5 5.3 %collective-permute-start.4 = (bf16[1,1,32,640]{3,2,1,0:T(8,128)(2,1)S(1)}, bf16[1,1,32,640]{3,2,1,0:T(8,128)(2,1)S(1)}, u32[]{:S(2)}, u32[]{:S(2)}) collective-permute-start(bf16[1,1,32,640]{3,2,1,0:T(8,128)(2,1)S(1)} %get-tuple-element.157), channel_id=1, source_target_pairs={{0,8},{8,16},{16,24},{24,32},{32,40},{40,48},{48,56},{56,64},{64,7... | collective-permute-start | bytes 122888 | tf_op jit(solution)/shard_map/ppermute | solution.py:19
  41.9 5.3 %collective-permute-start.5 = (bf16[1,1,32,640]{3,2,1,0:T(8,128)(2,1)S(1)}, bf16[1,1,32,640]{3,2,1,0:T(8,128)(2,1)S(1)}, u32[]{:S(2)}, u32[]{:S(2)}) collective-permute-start(bf16[1,1,32,640]{3,2,1,0:T(8,128)(2,1)S(1)} %get-tuple-element.158), channel_id=1, source_target_pairs={{8,0},{16,8},{24,16},{32,24},{40,32},{48,40},{56,48},{64,56},{72,6... | collective-permute-start | bytes 122888 | tf_op jit(solution)/shard_map/ppermute | solution.py:21
  47.2 5.8 %collective-permute-start.6 = (bf16[1,10,1,640]{3,2,1,0:T(2,128)(2,1)S(1)}, bf16[1,10,1,640]{3,2,1,0:T(2,128)(2,1)S(1)}, u32[]{:S(2)}, u32[]{:S(2)}) collective-permute-start(bf16[1,10,1,640]{3,2,1,0:T(2,128)(2,1)S(1)} %get-tuple-element.152), channel_id=1, source_target_pairs={{0,1},{1,2},{2,3},{3,4},{4,5},{5,6},{6,7},{8,9},{9,10},{10,11},{11... | collective-permute-start | bytes 38408 | tf_op jit(solution)/shard_map/ppermute | solution.py:19
  51.5 6.1 %collective-permute-start.7 = (bf16[1,10,1,640]{3,2,1,0:T(2,128)(2,1)S(1)}, bf16[1,10,1,640]{3,2,1,0:T(2,128)(2,1)S(1)}, u32[]{:S(2)}, u32[]{:S(2)}) collective-permute-start(bf16[1,10,1,640]{3,2,1,0:T(2,128)(2,1)S(1)} %get-tuple-element.151), channel_id=1, source_target_pairs={{1,0},{2,1},{3,2},{4,3},{5,4},{6,5},{7,6},{9,8},{10,9},{11,10},{12... | collective-permute-start | bytes 38408 | tf_op jit(solution)/shard_map/ppermute | solution.py:21
  57.8 2.2 slice-start
  58.3 2.8 slice-start.1
Sparse Core Ops, SparseCore 0:
  73.3 177.7 all-reduce.2
where the time goes:
time: 443 us; the launch traced here: 444 us
  waiting for transfers between devices  193 us (44%)
  matrix products  115 us (26%)
  blocking collectives  63.8 us (14%)
  starting transfers between devices  23.7 us (5%)
  between operations  17.5 us (4%)
  loops' own time  15 us (3%)
  local copies, waits for them, and re-layouts  11.8 us (3%)
  other arithmetic  4.89 us (1%)
    unnamed x2, waiting for transfers between devices  177 us
    dot_general x5, matrix products, accumulate(): jnp.dot(rows_now, block, preferred_element_type=jnp.float32, precision=la...  99.8 us
    psum x1, blocking collectives, on_device(): lax.psum(partial_sketch / math.sqrt(9.0 * channels * channels), ('row', '...  63.8 us
    ppermute x4, starting transfers between devices, extended(): lax.ppermute(tail, axis, [(i, (i + 1) % count) for i in range(ends)])  17 us
    ppermute x4, waiting for transfers between devices, extended(): lax.ppermute(head, axis, [((i + 1) % count, i) for i in range(ends)])  15.7 us
    another operation x1, loops' own time, on_device(): lax.fori_loop(0, owned, accumulate, jnp.zeros((batch, K), jnp.float32))  15 us
  transfers between devices with their start and end apart: 9, of which 5 were waited for; matrix products, arithmetic and copies ran while one was open for 0% of the time, Pallas kernels for 0%

commit v1 on v0

--- a/solution.py
+++ b/solution.py
@@ -1,11 +1,22 @@
+import functools
 import math
 
 import jax
 import jax.numpy as jnp
 from jax import lax
+from jax.experimental import pallas as pl
+from jax.experimental.pallas import tpu as pltpu
 from jax.sharding import PartitionSpec as P
 
 K = 1024
+M1 = 2146121005
+M2 = -2073254261
+MESH = pl.DeviceIdType.MESH
+
+
+def wrap32(value):
+    value &= 0xFFFFFFFF
+    return value - (1 << 32) if value >= (1 << 31) else value
 
 
 def extended(cells, sides, width):
@@ -27,23 +38,15 @@
 
 def mix_bits(value):
     value = value ^ lax.shift_right_logical(value, jnp.int32(16))
-    value = value * jnp.int32(2146121005)
+    value = value * jnp.int32(M1)
     value = value ^ lax.shift_right_logical(value, jnp.int32(15))
-    value = value * jnp.int32(-2073254261)
+    value = value * jnp.int32(M2)
     value = value ^ lax.shift_right_logical(value, jnp.int32(16))
     return value
 
 
 def noise_field(
-    example_ids,
-    noise_seed,
-    row_first,
-    col_first,
-    tile_rows,
-    tile_cols,
-    channels,
-    rows_all,
-    cols_all,
+    example_ids, noise_seed, row_first, col_first, tile_rows, tile_cols, channels, rows_all, cols_all
 ):
     row_ids = row_first + jnp.arange(tile_rows, dtype=jnp.int32)
     col_ids = col_first + jnp.arange(tile_cols, dtype=jnp.int32)
@@ -74,11 +77,310 @@
     return jnp.concatenate([jnp.sin(angles), jnp.cos(angles)], axis=1)
 
 
-def sign_block(first_index, width, proj_count, salt):
-    flat_ids = first_index + jnp.arange(width, dtype=jnp.int32)
-    column_ids = jnp.arange(proj_count, dtype=jnp.int32)
-    bits = mix_bits(flat_ids[:, None] * proj_count + column_ids[None, :] + salt)
-    return jnp.where(bits < 0, -1.0, 1.0).astype(jnp.float32)
+CH = 640
+TAPS = 9 * CH
+THIRD = 3 * CH
+CUT = 1024
+OWN = 5
+RUN = OWN * TAPS
+PADDED = 29184
+BLOCK = 1536
+ORDERS = (("x", "y", "z"), ("y", "z", "x"), ("z", "x", "y"))
+
+
+def place():
+    r = lax.axis_index("row")
+    c = lax.axis_index("col")
+    return {
+        "core": lax.rem(r, 2),
+        "x": lax.rem(r // 2, 4),
+        "y": lax.rem(c, 2) * 2 + r // 8,
+        "z": c // 2,
+    }
+
+
+def device(at, **moved):
+    at = {**at, **moved}
+    row = (lax.rem(at["y"], 2) * 4 + at["x"]) * 2 + at["core"]
+    return (row, at["z"] * 2 + at["y"] // 2)
+
+
+def hop(at, axis, by):
+    return lax.rem(at[axis] + (by + 4), 4)
+
+
+def peers_of(at):
+    out = []
+    for step in range(4):
+        for flip in range(2):
+            if step or flip:
+                out.append(device(at, x=hop(at, "x", step), core=lax.rem(at["core"] + flip, 2)))
+    for axis in ("y", "z"):
+        for step in range(1, 4):
+            out.append(device(at, **{axis: hop(at, axis, step)}))
+    return out
+
+
+def selection(third, core):
+    row = lax.broadcasted_iota(jnp.int32, (320, CH), 0)
+    owner = lax.shift_right_logical(row * 52429, jnp.int32(18))
+    channel = row - owner * OWN
+    digits = (lax.shift_right_logical(owner, jnp.int32(4)), lax.shift_right_logical(owner, jnp.int32(2)) & 3, owner & 3)
+    named = dict(zip(ORDERS[third], digits))
+    wanted = ((core * 4 + named["x"]) * 4 + named["y"]) * 4 + named["z"]
+    wanted = wanted * OWN + channel
+    lane = lax.broadcasted_iota(jnp.int32, (320, CH), 1)
+    return jnp.where(lane == wanted, 1.0, 0.0).astype(jnp.bfloat16)
+
+
+def f32(value):
+    return value.astype(jnp.float32)
+
+
+def project(salt, first, row, grow, acc):
+    q = lax.shift_right_logical(salt, jnp.int32(10))
+    s = salt & (K - 1)
+    m_first = (first + q) & jnp.int32((1 << 22) - 1)
+    ahead = m_first & 255
+    h_first = lax.shift_right_logical(m_first - ahead, jnp.int32(6))
+    flat = row[...]
+    whole = jnp.sum(flat)
+    one = pltpu.roll(flat, ahead, axis=1)
+    two = pltpu.roll(one, 1, axis=1)
+    one_hi = one.astype(jnp.bfloat16)
+    two_hi = two.astype(jnp.bfloat16)
+    one_lo = (one - f32(one_hi)).astype(jnp.bfloat16)
+    two_lo = (two - f32(two_hi)).astype(jnp.bfloat16)
+    none = jnp.zeros((4, PADDED), jnp.bfloat16)
+    grow[...] = jnp.concatenate([one_hi, two_hi, one_lo, two_lo, none], axis=0)
+    acc[...] = jnp.zeros_like(acc)
+    j = lax.broadcasted_iota(jnp.int32, (1, K), 1)
+    m_row = lax.broadcasted_iota(jnp.int32, (64, 1), 0)
+
+    def body(step, carry):
+        h_block = h_first + step * (BLOCK // 64)
+        parts = []
+        for part in range(BLOCK // 64):
+            if part % 4 == 0:
+                h_four = (h_block + part) & 65535
+                column = (m_row ^ lax.shift_right_logical(h_four, jnp.int32(10))) * jnp.int32(
+                    wrap32(1024 * M1)
+                )
+            h = h_four + part % 4
+            line = (j ^ (h & 1023)) * jnp.int32(M1) + h * jnp.int32(wrap32(65536 * M1))
+            w = line + column
+            y = (w ^ lax.shift_right_logical(w, jnp.int32(15))) * jnp.int32(M2)
+            parts.append(jnp.where(y < 0, 1.0, 0.0).astype(jnp.bfloat16))
+        signs = jnp.concatenate(parts, axis=0)
+        lanes = pl.ds(pl.multiple_of(step * BLOCK, BLOCK), BLOCK)
+        acc[...] += jnp.dot(grow[:, lanes], signs, preferred_element_type=jnp.float32)
+        return carry
+
+    lax.fori_loop(0, PADDED // BLOCK, body, 0)
+    here = whole - 2.0 * (acc[0:1, :] + acc[2:3, :])
+    past = whole - 2.0 * (acc[1:2, :] + acc[3:4, :])
+    return pltpu.roll(jnp.where(j >= s, here, past), (K - s) & (K - 1), axis=1)
+
+
+def back_kernel(
+    salt_ref, cot_ref, hid_ref, out_ref,
+    cot_far, hid_far, lhs, s1, r1a, r1b, r1, f2, s2, r2a, r2b, r2, f3, r3, row, grow, acc,
+    sum8, sum4, sum4b,
+    pair_send, pair_recv, ring_send, ring_recv, tail_send, tail_recv, all_send, all_recv,
+):
+    at = place()
+    peers = peers_of(at)
+    barrier = pltpu.get_barrier_semaphore()
+    for peer in peers:
+        pl.semaphore_signal(barrier, inc=1, device_id=peer, device_id_type=MESH)
+    pl.semaphore_wait(barrier, len(peers))
+
+    def send(src, dst, send_sem, recv_sem, to):
+        copy = pltpu.make_async_remote_copy(
+            src_ref=src, dst_ref=dst, send_sem=send_sem, recv_sem=recv_sem,
+            device_id=to, device_id_type=MESH,
+        )
+        copy.start()
+        return copy
+
+    partner = device(at, core=lax.rem(at["core"] + 1, 2))
+    pair = [
+        send(cot_ref, cot_far, pair_send.at[0], pair_recv.at[0], partner),
+        send(hid_ref, hid_far, pair_send.at[1], pair_recv.at[1], partner),
+    ]
+    pair[0].wait_recv()
+    for third in range(3):
+        pick = selection(third, at["core"])
+        for side, cot in enumerate((cot_ref, cot_far)):
+            lhs[third, side] = lax.dot_general(
+                pick, cot[...], (((1,), (1,)), ((), ())), preferred_element_type=jnp.float32
+            ).astype(jnp.bfloat16)
+    pair[1].wait_recv()
+
+    def ring_one(third, level, blocks, ra, rb):
+        axis = ORDERS[third][level]
+        mine = at[axis]
+        up = device(at, **{axis: hop(at, axis, 1)})
+        down = device(at, **{axis: hop(at, axis, -1)})
+        across = hop(at, axis, 2)
+        sems = (third, level)
+        return [
+            send(blocks.at[third, across, :, pl.ds(0, CUT)], ra.at[third],
+                 ring_send.at[third, level, 0], ring_recv.at[third, level, 0], up),
+            send(blocks.at[third, across, :, pl.ds(CUT, THIRD - CUT)], rb.at[third],
+                 ring_send.at[third, level, 1], ring_recv.at[third, level, 1], down),
+        ]
+
+    def ring_two(third, level, blocks, ra, rb, first, landed):
+        axis = ORDERS[third][level]
+        above = hop(at, axis, 1)
+        below = hop(at, axis, -1)
+        first[0].wait_recv()
+        old = blocks[third, above, :, 0:CUT]
+        blocks[third, above, :, 0:CUT] = (f32(old) + f32(ra[third])).astype(jnp.bfloat16)
+        up = send(blocks.at[third, above], landed.at[third, 0],
+                  ring_send.at[third, level, 2], ring_recv.at[third, level, 2],
+                  device(at, **{axis: above}))
+        first[1].wait_recv()
+        old = blocks[third, below, :, CUT:THIRD]
+        blocks[third, below, :, CUT:THIRD] = (f32(old) + f32(rb[third])).astype(jnp.bfloat16)
+        down = send(blocks.at[third, below], landed.at[third, 1],
+                    ring_send.at[third, level, 3], ring_recv.at[third, level, 3],
+                    device(at, **{axis: below}))
+        return [up, down]
+
+    started = list(pair)
+    ones = []
+    for third in range(3):
+        for dx in range(3):
+            near = hid_ref[dx, third : third + 8].reshape(256, CH)
+            far = hid_far[dx, third : third + 8].reshape(256, CH)
+            total = jnp.dot(lhs[third, 0], near, preferred_element_type=jnp.float32)
+            total += jnp.dot(lhs[third, 1], far, preferred_element_type=jnp.float32)
+            s1[third, :, :, dx * CH : (dx + 1) * CH] = total.astype(jnp.bfloat16).reshape(4, 80, CH)
+        ones.append(ring_one(third, 0, s1, r1a, r1b))
+    twos = [ring_two(t, 0, s1, r1a, r1b, ones[t], r1) for t in range(3)]
+    started += [copy for group in ones + twos for copy in group]
+    ones = []
+    for third in range(3):
+        mine = at[ORDERS[third][0]]
+        for copy in twos[third]:
+            copy.wait_recv()
+        total = f32(s1[third, mine]) + f32(r1[third, 0]) + f32(r1[third, 1])
+        for block in range(4):
+            piece = total[block * 20 : block * 20 + 20]
+            f2[third, block, 0:20] = piece
+            s2[third, block] = jnp.concatenate([piece, jnp.zeros((12, THIRD), jnp.float32)], axis=0).astype(
+                jnp.bfloat16
+            )
+        ones.append(ring_one(third, 1, s2, r2a, r2b))
+    twos = [ring_two(t, 1, s2, r2a, r2b, ones[t], r2) for t in range(3)]
+    started += [copy for group in ones + twos for copy in group]
+    lasts = []
+    for third in range(3):
+        mine = at[ORDERS[third][1]]
+        for copy in twos[third]:
+            copy.wait_recv()
+        total = f2[third, mine, 0:20] + f32(r2[third, 0, 0:20]) + f32(r2[third, 1, 0:20])
+        for block in range(4):
+            f3[third, block] = jnp.concatenate(
+                [total[block * OWN : (block + 1) * OWN], jnp.zeros((3, THIRD), jnp.float32)], axis=0
+            )
+        axis = ORDERS[third][2]
+        group = []
+        for step in range(1, 4):
+            to = hop(at, axis, step)
+            group.append(
+                send(f3.at[third, to], r3.at[third, step - 1],
+                     tail_send.at[third, step - 1], tail_recv.at[third, step - 1],
+                     device(at, **{axis: to}))
+            )
+        lasts.append(group)
+    row[...] = jnp.zeros_like(row)
+    for third in range(3):
+        mine = at[ORDERS[third][2]]
+        for copy in lasts[third]:
+            copy.wait_recv()
+        started += lasts[third]
+        total = f3[third, mine] + r3[third, 0] + r3[third, 1] + r3[third, 2]
+        for channel in range(OWN):
+            lanes = pl.ds(channel * TAPS + third * THIRD, THIRD)
+            row[0:1, lanes] = total[channel : channel + 1]
+
+    owner = ((at["core"] * 4 + at["x"]) * 4 + at["y"]) * 4 + at["z"]
+    share = project(salt_ref[0], owner * RUN, row, grow, acc)
+
+    share = share * (1.0 / math.sqrt(9.0 * CH * CH))
+    me = at["x"] * 2 + at["core"]
+    sum8[me] = share
+    group = []
+    for index, peer in enumerate(peers[:7]):
+        group.append(send(sum8.at[me], sum8.at[me], all_send.at[index], all_recv.at[index], peer))
+    for copy in group:
+        copy.wait_recv()
+    started += group
+    share = sum8[0]
+    for index in range(1, 8):
+        share = share + sum8[index]
+    for axis, slots, base in (("y", sum4, 7), ("z", sum4b, 10)):
+        me = at[axis]
+        slots[me] = share
+        group = []
+        for index in range(3):
+            group.append(send(slots.at[me], slots.at[me], all_send.at[base + index],
+                              all_recv.at[base + index], peers[base + index]))
+        for copy in group:
+            copy.wait_recv()
+        started += group
+        share = slots[0] + slots[1] + slots[2] + slots[3]
+    out_ref[...] = share
+    for copy in started:
+        copy.wait_send()
+
+
+def back(salt, cot, hid):
+    bf16, full = jnp.bfloat16, jnp.float32
+    vmem = pltpu.VMEM
+    dma = pltpu.SemaphoreType.DMA
+    return pl.pallas_call(
+        back_kernel,
+        out_shape=jax.ShapeDtypeStruct((1, K), full),
+        in_specs=[
+            pl.BlockSpec(memory_space=pltpu.SMEM),
+            pl.BlockSpec(memory_space=pltpu.VMEM),
+            pl.BlockSpec(memory_space=pltpu.VMEM),
+        ],
+        out_specs=pl.BlockSpec(memory_space=pltpu.VMEM),
+        scratch_shapes=[
+            vmem((256, CH), bf16),
+            vmem((3, 10, 32, CH), bf16),
+            vmem((3, 2, 320, 256), bf16),
+            vmem((3, 4, 80, THIRD), bf16),
+            vmem((3, 80, CUT), bf16),
+            vmem((3, 80, THIRD - CUT), bf16),
+            vmem((3, 2, 80, THIRD), bf16),
+            vmem((3, 4, 24, THIRD), full),
+            vmem((3, 4, 32, THIRD), bf16),
+            vmem((3, 32, CUT), bf16),
+            vmem((3, 32, THIRD - CUT), bf16),
+            vmem((3, 2, 32, THIRD), bf16),
+            vmem((3, 4, 8, THIRD), full),
+            vmem((3, 3, 8, THIRD), full),
+            vmem((1, PADDED), full),
+            vmem((8, PADDED), bf16),
+            vmem((8, K), full),
+            vmem((8, 1, K), full),
+            vmem((4, 1, K), full),
+            vmem((4, 1, K), full),
+            dma((2,)), dma((2,)),
+            dma((3, 2, 4)), dma((3, 2, 4)),
+            dma((3, 3)), dma((3, 3)),
+            dma((13,)), dma((13,)),
+        ],
+        compiler_params=pltpu.CompilerParams(
+            collective_id=0, has_side_effects=True, vmem_limit_bytes=56 * 2**20
+        ),
+    )(salt, cot, hid)
 
 
 def unfold(padded, tile_rows, tile_cols):
@@ -103,15 +405,7 @@
     row_first = lax.axis_index("row") * tile_rows
     col_first = lax.axis_index("col") * tile_cols
     noise = noise_field(
-        example_ids,
-        noise_seed,
-        row_first,
-        col_first,
-        tile_rows,
-        tile_cols,
-        channels,
-        rows_all,
-        cols_all,
+        example_ids, noise_seed, row_first, col_first, tile_rows, tile_cols, channels, rows_all, cols_all
     )
     abar = plan(timestep)[:, None, None, None]
     noisy = (jnp.sqrt(abar) * latent.astype(jnp.float32) + jnp.sqrt(1.0 - abar) * noise).astype(
@@ -138,29 +432,10 @@
     out_full = noisy.astype(jnp.float32) + conv_out.reshape(batch, tile_rows, tile_cols, channels)
     section_out = out_full.astype(jnp.bfloat16)
     cot = ((out_full - noise) / math.sqrt(rows_all * cols_all)).astype(jnp.bfloat16)
-    cot = cot.reshape(batch, tile_rows * tile_cols, channels)
-    owned = channels // (rows_count * cols_count)
-    value = jnp.einsum("bpo,bpq->obq", cot, hid_cols, preferred_element_type=jnp.float32)
-    grad = lax.psum_scatter(
-        value.reshape(lax.axis_size(("row", "col")) * owned, batch * 9 * channels),
-        ("row", "col"),
-        scatter_dimension=0,
-        tiled=True,
-    )
-    chan_first = (lax.axis_index("row") * cols_count + lax.axis_index("col")) * owned
-    grad = grad.reshape(owned, batch, 9 * channels)
-    salt = mix_bits(proj_seed[0] + jnp.int32(12345))
-
-    def accumulate(step, total):
-        out_chan = chan_first + step
-        block = sign_block(out_chan * (9 * channels), 9 * channels, K, salt)
-        rows_now = lax.dynamic_slice_in_dim(grad, step, 1, 0)[0]
-        return total + jnp.dot(
-            rows_now, block, preferred_element_type=jnp.float32, precision=lax.Precision.HIGHEST
-        )
-
-    partial_sketch = lax.fori_loop(0, owned, accumulate, jnp.zeros((batch, K), jnp.float32))
-    sketch = lax.psum(partial_sketch / math.sqrt(9.0 * channels * channels), ("row", "col"))
+    cot = cot.reshape(batch * tile_rows * tile_cols, channels)
+    shifted = jnp.stack([hid_pad[0, :, dx : dx + tile_cols, :] for dx in range(3)])
+    salt = mix_bits(proj_seed + jnp.int32(12345))
+    sketch = back(salt, cot, shifted)
     return (section_out, sketch)
 
 

time: 443 us -> 146 us (0.33)
  waiting for transfers between devices: 193 us -> 2.79 us
  matrix products: 115 us -> 7.26 us
  Pallas kernels: 0 us -> 93.3 us
  blocking collectives: 63.8 us -> 0 us
  loops' own time: 15 us -> 0 us
  between operations: 17.5 us -> 3.81 us
  local copies, waits for them, and re-layouts: 11.8 us -> 3.21 us
  starting transfers between devices: 23.7 us -> 28.5 us
    unnamed x2 -> x0, waiting for transfers between devices: 177 us -> none
    dot_general x6 -> x0, matrix products: 107 us -> none  [the longest x5 99.8 us: accumulate(): jnp.dot(rows_now, block, preferred_element_type=jnp.float32, precision=la...]
    pallas_call x0 -> x1, Pallas kernels: none -> 93.3 us  [back(): pl.pallas_call(back_kernel, out_shape=jax.ShapeDtypeStruct((1, K), full),...]
    psum x1 -> x0, blocking collectives: 63.8 us -> none  [on_device(): lax.psum(partial_sketch / math.sqrt(9.0 * channels * channels), ('row', '...]
    ppermute x4, waiting for transfers between devices: 15.7 us -> 0.01 us  [extended(): lax.ppermute(head, axis, [((i + 1) % count, i) for i in range(ends)])]
    another operation x1 -> x0, loops' own time: 15 us -> none  [on_device(): lax.fori_loop(0, owned, accumulate, jnp.zeros((batch, K), jnp.float32))]
    reshape x1 -> x0, local copies, waits for them, and re-layouts: 5.08 us -> none  [on_device(): grad = grad.reshape(owned, batch, 9 * channels)]
  transfers between devices with their start and end apart: 9 -> 8, of which waited for: 5 -> 4; matrix products, arithmetic and copies ran while one was open for 0% -> 0% of each run, Pallas kernels for 0% -> 0%
where the time goes in v1:
time: 146 us; the launch traced here: 145 us
  Pallas kernels  93.3 us (64%)
  starting transfers between devices  28.5 us (20%)
  matrix products  7.26 us (5%)
  other arithmetic  6.03 us (4%)
  between operations  3.81 us (3%)
  local copies, waits for them, and re-layouts  3.21 us (2%)
  waiting for transfers between devices  2.79 us (2%)
    pallas_call x1, Pallas kernels, back(): pl.pallas_call(back_kernel, out_shape=jax.ShapeDtypeStruct((1, K), full),...  93.3 us
    ppermute x4, starting transfers between devices, extended(): lax.ppermute(tail, axis, [(i, (i + 1) % count) for i in range(ends)])  20.3 us
    ppermute x4, starting transfers between devices, extended(): lax.ppermute(head, axis, [((i + 1) % count, i) for i in range(ends)])  8.18 us
    dot_general x1, matrix products, on_device(): jnp.dot(hid_cols.reshape(batch * tile_rows * tile_cols, 9 * channels), co...  4.51 us
  transfers between devices with their start and end apart: 8, of which 4 were waited for; matrix products, arithmetic and copies ran while one was open for 0% of the time, Pallas kernels for 0%

profile of v1, /device:TPU:1, one launch (start us, length us, event | category | flops | bytes accessed | tf_op | source)
XLA Modules:
  0.0 144.8 jit_solution(2010077604873222055)
XLA Ops:
  2.9 2.4 %fusion.45 = bf16[1,8,32,640]{3,2,1,0:T(8,128)(2,1)S(1)} fusion(f32[]{:T(128)} %bitcast.3, s32[]{:T(128)S(6)} %xor.200, s32[8,32]{1,0:T(8,128)S(1)} %add_multiply_fusion, bf16[1,8,32,640]{3,2,1,0:T(8,128)(2,1)} %param.8, f32[]{:T(128)} %bitcast), kind=kLoop, calls=%fused_computation.49 | loop fusion | flops 10649600 | bytes 656396 | tf_op jit(solution)/shard_map/convert_element_type | solution.py:414
  5.4 3.5 %collective-permute-start.1 = (bf16[1,1,32,640]{3,2,1,0:T(8,128)(2,1)S(1)}, bf16[1,1,32,640]{3,2,1,0:T(8,128)(2,1)S(1)}, u32[]{:S(2)}, u32[]{:S(2)}) collective-permute-start(bf16[1,1,32,640]{3,2,1,0:T(8,128)(2,1)S(1)} %get-tuple-element.15), channel_id=1, source_target_pairs={{8,0},{16,8},{24,16},{32,24},{40,32},{48,40},{56,48},{64,56},{72,6... | collective-permute-start | bytes 122888 | tf_op jit(solution)/shard_map/ppermute | solution.py:32
  8.9 3.1 %collective-permute-start = (bf16[1,1,32,640]{3,2,1,0:T(8,128)(2,1)S(1)}, bf16[1,1,32,640]{3,2,1,0:T(8,128)(2,1)S(1)}, u32[]{:S(2)}, u32[]{:S(2)}) collective-permute-start(bf16[1,1,32,640]{3,2,1,0:T(8,128)(2,1)S(1)} %get-tuple-element.14), channel_id=1, source_target_pairs={{0,8},{8,16},{16,24},{24,32},{32,40},{40,48},{48,56},{56,64},{64,7... | collective-permute-start | bytes 122888 | tf_op jit(solution)/shard_map/ppermute | solution.py:30
  12.1 0.9 collective-permute-done
  13.1 1.3 collective-permute-start.3
  14.4 5.5 %collective-permute-start.2 = (bf16[1,10,1,640]{3,2,1,0:T(2,128)(2,1)S(1)}, bf16[1,10,1,640]{3,2,1,0:T(2,128)(2,1)S(1)}, u32[]{:S(2)}, u32[]{:S(2)}) collective-permute-start(bf16[1,10,1,640]{3,2,1,0:T(2,128)(2,1)S(1)} %get-tuple-element.11), channel_id=1, source_target_pairs={{0,1},{1,2},{2,3},{3,4},{4,5},{5,6},{6,7},{8,9},{9,10},{10,11},{11... | collective-permute-start | bytes 38408 | tf_op jit(solution)/shard_map/ppermute | solution.py:30
  19.9 0.2 convolution_reduce_fusion
  20.1 0.7 collective-permute-done.2
  20.8 0.2 pad_maximum_fusion.1
  21.3 1.5 %constant_dynamic-update-slice_fusion = bf16[1,8,32,5760]{3,2,1,0:T(8,128)(2,1)S(1)} fusion(bf16[1,8,32,5760]{3,2,1,0:T(8,128)(2,1)S(1)} %slice_dynamic-update-slice_fusion.9, f32[]{:T(128)} %bitcast.3, s32[]{:T(128)S(6)} %xor.200, s32[8,32]{1,0:T(8,128)S(1)} %add_multiply_fusion, bf16[1,8,32,640]{3,2,1,0:T(8,128)(2,1)S(1)} %copy-done.1, f32[]{:T(128)} %bitcast), kind=kLoop, calls=%fused_computation.78 | loop fusion | flops 10649600 | bytes 659468
  22.8 0.1 slice_dynamic-update-slice_fusion.8
  23.0 0.1 slice_dynamic-update-slice_fusion.6
  23.1 0.8 copy-done.2
  23.9 2.5 %fusion.50 = bf16[1,8,32,640]{3,2,1,0:T(8,128)(2,1)S(1)} fusion(bf16[5760,640]{1,0:T(8,128)(2,1)S(1)} %copy-done.2, bf16[1,8,32,5760]{3,2,1,0:T(8,128)(2,1)S(1)} %slice_dynamic-update-slice_fusion.6, f32[640]{0:T(1024)S(1)} %convolution_reduce_fusion), kind=kOutput, calls=%fused_computation.52 | convolution fusion | flops 1888419840 | bytes 10652160 | tf_op jit(solution)/shard_map/dot_general | solution.py:421
  26.5 2.1 %collective-permute-start.5 = (bf16[1,1,32,640]{3,2,1,0:T(8,128)(2,1)S(1)}, bf16[1,1,32,640]{3,2,1,0:T(8,128)(2,1)S(1)}, u32[]{:S(2)}, u32[]{:S(2)}) collective-permute-start(bf16[1,1,32,640]{3,2,1,0:T(8,128)(2,1)S(1)} %get-tuple-element.13), channel_id=1, source_target_pairs={{8,0},{16,8},{24,16},{32,24},{40,32},{48,40},{56,48},{64,56},{72,6... | collective-permute-start | bytes 122888 | tf_op jit(solution)/shard_map/ppermute | solution.py:32
  28.6 5.2 %collective-permute-start.4 = (bf16[1,1,32,640]{3,2,1,0:T(8,128)(2,1)S(1)}, bf16[1,1,32,640]{3,2,1,0:T(8,128)(2,1)S(1)}, u32[]{:S(2)}, u32[]{:S(2)}) collective-permute-start(bf16[1,1,32,640]{3,2,1,0:T(8,128)(2,1)S(1)} %get-tuple-element.12), channel_id=1, source_target_pairs={{0,8},{8,16},{16,24},{24,32},{32,40},{40,48},{48,56},{56,64},{64,7... | collective-permute-start | bytes 122888 | tf_op jit(solution)/shard_map/ppermute | solution.py:30
  33.8 1.1 collective-permute-done.4
  34.9 1.3 collective-permute-start.7
  36.2 6.5 %collective-permute-start.6 = (bf16[1,10,1,640]{3,2,1,0:T(2,128)(2,1)S(1)}, bf16[1,10,1,640]{3,2,1,0:T(2,128)(2,1)S(1)}, u32[]{:S(2)}, u32[]{:S(2)}) collective-permute-start(bf16[1,10,1,640]{3,2,1,0:T(2,128)(2,1)S(1)} %get-tuple-element.7), channel_id=1, source_target_pairs={{0,1},{1,2},{2,3},{3,4},{4,5},{5,6},{6,7},{8,9},{9,10},{10,11},{11... | collective-permute-start | bytes 38408 | tf_op jit(solution)/shard_map/ppermute | solution.py:30
  43.5 0.2 pad_maximum_fusion.2
  44.5 4.5 %multiply_convert_fusion = (bf16[1,8,32,640]{3,2,1,0:T(8,128)(2,1)}, bf16[1,8,32,640]{3,2,1,0:T(8,128)(2,1)}) fusion(s32[]{:T(128)S(6)} %xor.200, s32[8,32]{1,0:T(8,128)S(1)} %add_multiply_fusion, bf16[5760,640]{1,0:T(8,128)(2,1)S(1)} %bitcast.54, bf16[1,8,32,5760]{3,2,1,0:T(8,128)(2,1)S(1)} %slice_dynamic-update-slice_fusion, f32[]{:T(128)} %bitcast.3, ...), kind=kOutput, calls=%fused_computation.50 | convolution fusion | flops 1898250240 | bytes 11305996 | tf_op jit(solution)/shard_map/dot_general | solution.py:427
  49.0 1.2 pad_maximum_fusion.hid_ref
  50.3 93.3 %shard_map.95 = f32[1,1024]{1,0:T(1,128)} custom-call(s32[1]{0:T(128)S(6)} %xor.215.salt_ref, bf16[256,640]{1,0:T(8,128)(2,1)} %bitcast.52, bf16[3,10,32,640]{3,2,1,0:T(8,128)(2,1)} %pad_maximum_fusion.hid_ref), custom_call_target="tpu_custom_call" | custom-call | tf_op jit(solution)/shard_map/pallas_call | solution.py:345
  143.5 1.3 copy.31
  (42 shorter events, 1.5 us)
Async XLA Ops:
  0.6 19.3 %copy-start = (bf16[640,640]{1,0:T(8,128)(2,1)S(1)}, bf16[640,640]{1,0:T(8,128)(2,1)}, u32[]{:S(2)}) copy-start(bf16[640,640]{1,0:T(8,128)(2,1)} %param.13) | copy-start | bytes 2457604
  5.4 15.9 %copy-start.1 = (bf16[1,8,32,640]{3,2,1,0:T(8,128)(2,1)S(1)}, bf16[1,8,32,640]{3,2,1,0:T(8,128)(2,1)}, u32[]{:S(2)}) copy-start(bf16[1,8,32,640]{3,2,1,0:T(8,128)(2,1)} %param.8) | copy-start | bytes 983044
  5.4 6.7 %collective-permute-start.1 = (bf16[1,1,32,640]{3,2,1,0:T(8,128)(2,1)S(1)}, bf16[1,1,32,640]{3,2,1,0:T(8,128)(2,1)S(1)}, u32[]{:S(2)}, u32[]{:S(2)}) collective-permute-start(bf16[1,1,32,640]{3,2,1,0:T(8,128)(2,1)S(1)} %get-tuple-element.15), channel_id=1, source_target_pairs={{8,0},{16,8},{24,16},{32,24},{40,32},{48,40},{56,48},{64,56},{72,6... | collective-permute-start | bytes 122888 | tf_op jit(solution)/shard_map/ppermute | solution.py:32
  8.9 4.2 %collective-permute-start = (bf16[1,1,32,640]{3,2,1,0:T(8,128)(2,1)S(1)}, bf16[1,1,32,640]{3,2,1,0:T(8,128)(2,1)S(1)}, u32[]{:S(2)}, u32[]{:S(2)}) collective-permute-start(bf16[1,1,32,640]{3,2,1,0:T(8,128)(2,1)S(1)} %get-tuple-element.14), channel_id=1, source_target_pairs={{0,8},{8,16},{16,24},{24,32},{32,40},{40,48},{48,56},{56,64},{64,7... | collective-permute-start | bytes 122888 | tf_op jit(solution)/shard_map/ppermute | solution.py:30
  13.1 7.0 %collective-permute-start.3 = (bf16[1,10,1,640]{3,2,1,0:T(2,128)(2,1)S(1)}, bf16[1,10,1,640]{3,2,1,0:T(2,128)(2,1)S(1)}, u32[]{:S(2)}, u32[]{:S(2)}) collective-permute-start(bf16[1,10,1,640]{3,2,1,0:T(2,128)(2,1)S(1)} %get-tuple-element.10), channel_id=1, source_target_pairs={{1,0},{2,1},{3,2},{4,3},{5,4},{6,5},{7,6},{9,8},{10,9},{11,10},{12... | collective-permute-start | bytes 38408 | tf_op jit(solution)/shard_map/ppermute | solution.py:32
  14.4 6.4 %collective-permute-start.2 = (bf16[1,10,1,640]{3,2,1,0:T(2,128)(2,1)S(1)}, bf16[1,10,1,640]{3,2,1,0:T(2,128)(2,1)S(1)}, u32[]{:S(2)}, u32[]{:S(2)}) collective-permute-start(bf16[1,10,1,640]{3,2,1,0:T(2,128)(2,1)S(1)} %get-tuple-element.11), channel_id=1, source_target_pairs={{0,1},{1,2},{2,3},{3,4},{4,5},{5,6},{6,7},{8,9},{9,10},{10,11},{11... | collective-permute-start | bytes 38408 | tf_op jit(solution)/shard_map/ppermute | solution.py:30
  20.8 3.1 %copy-start.2 = (bf16[5760,640]{1,0:T(8,128)(2,1)S(1)}, bf16[5760,640]{1,0:T(8,128)(2,1)}, u32[]{:S(2)}) copy-start(bf16[5760,640]{1,0:T(8,128)(2,1)} %param.14) | copy-start | bytes 22118404
  23.0 21.5 %slice-start = ((s8[7372800]{0:T(1024)(128)(4,1)}), s8[4194304]{0:T(1024)(128)(4,1)S(1)}, s32[]{:S(2)}) async-start(s8[7372800]{0:T(1024)(128)(4,1)} %bitcast.53), calls=%async_computation | async-start | bytes 8388608
  23.9 20.6 %slice-start.1 = ((s8[7372800]{0:T(1024)(128)(4,1)}), s8[3178496]{0:T(1024)(128)(4,1)S(1)}, s32[]{:S(2)}) async-start(s8[7372800]{0:T(1024)(128)(4,1)} %bitcast.53), calls=%async_computation.1 | async-start | bytes 6356992
  26.5 7.3 %collective-permute-start.5 = (bf16[1,1,32,640]{3,2,1,0:T(8,128)(2,1)S(1)}, bf16[1,1,32,640]{3,2,1,0:T(8,128)(2,1)S(1)}, u32[]{:S(2)}, u32[]{:S(2)}) collective-permute-start(bf16[1,1,32,640]{3,2,1,0:T(8,128)(2,1)S(1)} %get-tuple-element.13), channel_id=1, source_target_pairs={{8,0},{16,8},{24,16},{32,24},{40,32},{48,40},{56,48},{64,56},{72,6... | collective-permute-start | bytes 122888 | tf_op jit(solution)/shard_map/ppermute | solution.py:32
  28.6 6.2 %collective-permute-start.4 = (bf16[1,1,32,640]{3,2,1,0:T(8,128)(2,1)S(1)}, bf16[1,1,32,640]{3,2,1,0:T(8,128)(2,1)S(1)}, u32[]{:S(2)}, u32[]{:S(2)}) collective-permute-start(bf16[1,1,32,640]{3,2,1,0:T(8,128)(2,1)S(1)} %get-tuple-element.12), channel_id=1, source_target_pairs={{0,8},{8,16},{16,24},{24,32},{32,40},{40,48},{48,56},{56,64},{64,7... | collective-permute-start | bytes 122888 | tf_op jit(solution)/shard_map/ppermute | solution.py:30
  34.9 8.5 %collective-permute-start.7 = (bf16[1,10,1,640]{3,2,1,0:T(2,128)(2,1)S(1)}, bf16[1,10,1,640]{3,2,1,0:T(2,128)(2,1)S(1)}, u32[]{:S(2)}, u32[]{:S(2)}) collective-permute-start(bf16[1,10,1,640]{3,2,1,0:T(2,128)(2,1)S(1)} %get-tuple-element.6), channel_id=1, source_target_pairs={{1,0},{2,1},{3,2},{4,3},{5,4},{6,5},{7,6},{9,8},{10,9},{11,10},{12... | collective-permute-start | bytes 38408 | tf_op jit(solution)/shard_map/ppermute | solution.py:32
  36.2 7.3 %collective-permute-start.6 = (bf16[1,10,1,640]{3,2,1,0:T(2,128)(2,1)S(1)}, bf16[1,10,1,640]{3,2,1,0:T(2,128)(2,1)S(1)}, u32[]{:S(2)}, u32[]{:S(2)}) collective-permute-start(bf16[1,10,1,640]{3,2,1,0:T(2,128)(2,1)S(1)} %get-tuple-element.7), channel_id=1, source_target_pairs={{0,1},{1,2},{2,3},{3,4},{4,5},{5,6},{6,7},{8,9},{9,10},{10,11},{11... | collective-permute-start | bytes 38408 | tf_op jit(solution)/shard_map/ppermute | solution.py:30

commit v2 on v1

--- a/solution.py
+++ b/solution.py
@@ -9,6 +9,7 @@
 from jax.sharding import PartitionSpec as P
 
 K = 1024
+FILLS = (8, 16, 36, 10, 18)
 M1 = 2146121005
 M2 = -2073254261
 MESH = pl.DeviceIdType.MESH
@@ -84,7 +85,9 @@
 OWN = 5
 RUN = OWN * TAPS
 PADDED = 29184
-BLOCK = 1536
+BLOCK = 4864
+F8 = jnp.float8_e4m3fn
+PARTS = 4
 ORDERS = (("x", "y", "z"), ("y", "z", "x"), ("z", "x", "y"))
 
 
@@ -122,7 +125,7 @@
 
 
 def selection(third, core):
-    row = lax.broadcasted_iota(jnp.int32, (320, CH), 0)
+    row = lax.broadcasted_iota(jnp.int32, (320, 1), 0)
     owner = lax.shift_right_logical(row * 52429, jnp.int32(18))
     channel = row - owner * OWN
     digits = (lax.shift_right_logical(owner, jnp.int32(4)), lax.shift_right_logical(owner, jnp.int32(2)) & 3, owner & 3)
@@ -137,54 +140,77 @@
     return value.astype(jnp.float32)
 
 
-def project(salt, first, row, grow, acc):
-    q = lax.shift_right_logical(salt, jnp.int32(10))
+def shift_right(value, by):
+    return lax.shift_right_logical(value, jnp.int32(by))
+
+
+def alignment(salt, first):
+    m_first = (first + shift_right(salt, 10)) & jnp.int32((1 << 22) - 1)
+    ahead = m_first & 255
+    return ahead, shift_right(m_first - ahead, 6)
+
+
+def make_signs(salt, first, bits, low, high):
+    h_first = alignment(salt, first)[1]
+    lane = lax.broadcasted_iota(jnp.int32, (1, 128), 1)
+    m_row = lax.broadcasted_iota(jnp.int32, (32, 128), 0)
+
+    def body(step, carry):
+        h_four = (h_first + step * 4) & 65535
+        high_bits = shift_right(h_four, 10)
+        columns = [((m_row + half) ^ high_bits) * jnp.int32(wrap32(1024 * M1)) for half in (0, 32)]
+        for part in range(4):
+            h = h_four + part
+            for j in range(0, K, 128):
+                line = ((lane + j) ^ (h & 1023)) * jnp.int32(M1) + h * jnp.int32(wrap32(65536 * M1))
+                line = jnp.broadcast_to(line, (32, 128))
+                for half in range(2):
+                    w = line + columns[half]
+                    y = (w ^ shift_right(w, 15)) * jnp.int32(M2)
+                    rows = pl.ds(pl.multiple_of(step * 256 + part * 64 + half * 32, 32), 32)
+                    bits[rows, j : j + 128] = lax.shift_right_arithmetic(y, 31).astype(jnp.int8).astype(F8)
+        return carry
+
+    lax.fori_loop(low, high, body, 0)
+
+
+def project(salt, first, row, grow, bits, acc):
     s = salt & (K - 1)
-    m_first = (first + q) & jnp.int32((1 << 22) - 1)
-    ahead = m_first & 255
-    h_first = lax.shift_right_logical(m_first - ahead, jnp.int32(6))
+    ahead = alignment(salt, first)[0]
     flat = row[...]
     whole = jnp.sum(flat)
-    one = pltpu.roll(flat, ahead, axis=1)
+    largest = jnp.maximum(jnp.max(jnp.abs(flat)), 1e-30)
+    one = pltpu.roll(flat * (16.0 / largest), ahead, axis=1)
     two = pltpu.roll(one, 1, axis=1)
-    one_hi = one.astype(jnp.bfloat16)
-    two_hi = two.astype(jnp.bfloat16)
-    one_lo = (one - f32(one_hi)).astype(jnp.bfloat16)
-    two_lo = (two - f32(two_hi)).astype(jnp.bfloat16)
-    none = jnp.zeros((4, PADDED), jnp.bfloat16)
-    grow[...] = jnp.concatenate([one_hi, two_hi, one_lo, two_lo, none], axis=0)
+    for block in range(PADDED // BLOCK):
+        lanes = slice(block * BLOCK, (block + 1) * BLOCK)
+        pair = jnp.concatenate([one[:, lanes], two[:, lanes]], axis=0)
+        pieces = []
+        for _ in range(PARTS):
+            piece = lax.round(pair, lax.RoundingMethod.TO_NEAREST_EVEN)
+            pieces.append(piece)
+            pair = (pair - piece) * 32.0
+        pieces.append(jnp.zeros((24, BLOCK), jnp.float32))
+        grow[:, lanes] = jnp.concatenate(pieces, axis=0).astype(F8)
     acc[...] = jnp.zeros_like(acc)
+
+    def body(step, carry):
+        lanes = pl.ds(pl.multiple_of(step * BLOCK, BLOCK), BLOCK)
+        acc[...] += jnp.dot(grow[:, lanes], bits[lanes, :], preferred_element_type=jnp.float32)
+        return carry
+
+    lax.fori_loop(0, PADDED // BLOCK, body, 0)
+    total = acc[6:8, :]
+    for index in (2, 1, 0):
+        total = acc[2 * index : 2 * index + 2, :] + total * (1.0 / 32.0)
+    total = whole + total * (largest * (2.0 / 16.0))
     j = lax.broadcasted_iota(jnp.int32, (1, K), 1)
-    m_row = lax.broadcasted_iota(jnp.int32, (64, 1), 0)
-
-    def body(step, carry):
-        h_block = h_first + step * (BLOCK // 64)
-        parts = []
-        for part in range(BLOCK // 64):
-            if part % 4 == 0:
-                h_four = (h_block + part) & 65535
-                column = (m_row ^ lax.shift_right_logical(h_four, jnp.int32(10))) * jnp.int32(
-                    wrap32(1024 * M1)
-                )
-            h = h_four + part % 4
-            line = (j ^ (h & 1023)) * jnp.int32(M1) + h * jnp.int32(wrap32(65536 * M1))
-            w = line + column
-            y = (w ^ lax.shift_right_logical(w, jnp.int32(15))) * jnp.int32(M2)
-            parts.append(jnp.where(y < 0, 1.0, 0.0).astype(jnp.bfloat16))
-        signs = jnp.concatenate(parts, axis=0)
-        lanes = pl.ds(pl.multiple_of(step * BLOCK, BLOCK), BLOCK)
-        acc[...] += jnp.dot(grow[:, lanes], signs, preferred_element_type=jnp.float32)
-        return carry
-
-    lax.fori_loop(0, PADDED // BLOCK, body, 0)
-    here = whole - 2.0 * (acc[0:1, :] + acc[2:3, :])
-    past = whole - 2.0 * (acc[1:2, :] + acc[3:4, :])
-    return pltpu.roll(jnp.where(j >= s, here, past), (K - s) & (K - 1), axis=1)
+    return pltpu.roll(jnp.where(j >= s, total[0:1], total[1:2]), (K - s) & (K - 1), axis=1)
 
 
 def back_kernel(
     salt_ref, cot_ref, hid_ref, out_ref,
-    cot_far, hid_far, lhs, s1, r1a, r1b, r1, f2, s2, r2a, r2b, r2, f3, r3, row, grow, acc,
+    cot_far, hid_far, lhs, s1, r1a, r1b, r1, f2, s2, r2a, r2b, r2, f3, r3, row, grow, acc, bits,
     sum8, sum4, sum4b,
     pair_send, pair_recv, ring_send, ring_recv, tail_send, tail_recv, all_send, all_recv,
 ):
@@ -203,11 +229,23 @@
         copy.start()
         return copy
 
+    salt = salt_ref[0]
+    owner = ((at["core"] * 4 + at["x"]) * 4 + at["y"]) * 4 + at["z"]
+    marks = [0]
+
+    def fill(count):
+        low = marks[-1]
+        high = min(low + count, PADDED // 256)
+        marks.append(high)
+        if high > low:
+            make_signs(salt, owner * RUN, bits, low, high)
+
     partner = device(at, core=lax.rem(at["core"] + 1, 2))
     pair = [
         send(cot_ref, cot_far, pair_send.at[0], pair_recv.at[0], partner),
         send(hid_ref, hid_far, pair_send.at[1], pair_recv.at[1], partner),
     ]
+    fill(FILLS[0])
     pair[0].wait_recv()
     for third in range(3):
         pick = selection(third, at["core"])
@@ -259,8 +297,10 @@
             total += jnp.dot(lhs[third, 1], far, preferred_element_type=jnp.float32)
             s1[third, :, :, dx * CH : (dx + 1) * CH] = total.astype(jnp.bfloat16).reshape(4, 80, CH)
         ones.append(ring_one(third, 0, s1, r1a, r1b))
+    fill(FILLS[1])
     twos = [ring_two(t, 0, s1, r1a, r1b, ones[t], r1) for t in range(3)]
     started += [copy for group in ones + twos for copy in group]
+    fill(FILLS[2])
     ones = []
     for third in range(3):
         mine = at[ORDERS[third][0]]
@@ -274,8 +314,10 @@
                 jnp.bfloat16
             )
         ones.append(ring_one(third, 1, s2, r2a, r2b))
+    fill(FILLS[3])
     twos = [ring_two(t, 1, s2, r2a, r2b, ones[t], r2) for t in range(3)]
     started += [copy for group in ones + twos for copy in group]
+    fill(FILLS[4])
     lasts = []
     for third in range(3):
         mine = at[ORDERS[third][1]]
@@ -296,6 +338,7 @@
                      device(at, **{axis: to}))
             )
         lasts.append(group)
+    fill(PADDED)
     row[...] = jnp.zeros_like(row)
     for third in range(3):
         mine = at[ORDERS[third][2]]
@@ -307,8 +350,7 @@
             lanes = pl.ds(channel * TAPS + third * THIRD, THIRD)
             row[0:1, lanes] = total[channel : channel + 1]
 
-    owner = ((at["core"] * 4 + at["x"]) * 4 + at["y"]) * 4 + at["z"]
-    share = project(salt_ref[0], owner * RUN, row, grow, acc)
+    share = project(salt, owner * RUN, row, grow, bits, acc)
 
     share = share * (1.0 / math.sqrt(9.0 * CH * CH))
     me = at["x"] * 2 + at["core"]
@@ -367,8 +409,9 @@
             vmem((3, 4, 8, THIRD), full),
             vmem((3, 3, 8, THIRD), full),
             vmem((1, PADDED), full),
-            vmem((8, PADDED), bf16),
-            vmem((8, K), full),
+            vmem((32, PADDED), F8),
+            vmem((32, K), full),
+            vmem((PADDED, K), F8),
             vmem((8, 1, K), full),
             vmem((4, 1, K), full),
             vmem((4, 1, K), full),
@@ -378,7 +421,7 @@
             dma((13,)), dma((13,)),
         ],
         compiler_params=pltpu.CompilerParams(
-            collective_id=0, has_side_effects=True, vmem_limit_bytes=56 * 2**20
+            collective_id=0, has_side_effects=True, vmem_limit_bytes=60 * 2**20
         ),
     )(salt, cot, hid)
 

time: 146 us -> 125 us (0.86)
  Pallas kernels: 93.3 us -> 72.2 us
    pallas_call x1, Pallas kernels: 93.3 us -> 72.2 us  [back(): pl.pallas_call(back_kernel, out_shape=jax.ShapeDtypeStruct((1, K), full),...]
where the time goes in v2:
time: 125 us; the launch traced here: 124 us
  Pallas kernels  72.2 us (58%)
  starting transfers between devices  28.3 us (23%)
  matrix products  7.26 us (6%)
  other arithmetic  6.03 us (5%)
  between operations  3.81 us (3%)
  local copies, waits for them, and re-layouts  3.21 us (3%)
  waiting for transfers between devices  2.97 us (2%)
    pallas_call x1, Pallas kernels, back(): pl.pallas_call(back_kernel, out_shape=jax.ShapeDtypeStruct((1, K), full),...  72.2 us
    ppermute x4, starting transfers between devices, extended(): lax.ppermute(tail, axis, [(i, (i + 1) % count) for i in range(ends)])  20.1 us
    ppermute x4, starting transfers between devices, extended(): lax.ppermute(head, axis, [((i + 1) % count, i) for i in range(ends)])  8.18 us
    dot_general x1, matrix products, on_device(): jnp.dot(hid_cols.reshape(batch * tile_rows * tile_cols, 9 * channels), co...  4.51 us
    ppermute x4, waiting for transfers between devices, extended(): lax.ppermute(tail, axis, [(i, (i + 1) % count) for i in range(ends)])  2.96 us
    unnamed x22, local copies, waits for them, and re-layouts  2.82 us
    dot_general x1, matrix products, on_device(): jnp.dot(act_cols, conv1_weight, preferred_element_type=jnp.float32)  2.52 us
  transfers between devices with their start and end apart: 8, of which 4 were waited for; matrix products, arithmetic and copies ran while one was open for 0% of the time, Pallas kernels for 0%

profile of v2, /device:TPU:1, one launch (start us, length us, event | category | flops | bytes accessed | tf_op | source)
XLA Modules:
  0.0 123.8 jit_solution(5628683131321088019)
XLA Ops:
  2.9 2.4 %fusion.45 = bf16[1,8,32,640]{3,2,1,0:T(8,128)(2,1)S(1)} fusion(f32[]{:T(128)} %bitcast.3, s32[]{:T(128)S(6)} %xor.200, s32[8,32]{1,0:T(8,128)S(1)} %add_multiply_fusion, bf16[1,8,32,640]{3,2,1,0:T(8,128)(2,1)} %param.8, f32[]{:T(128)} %bitcast), kind=kLoop, calls=%fused_computation.49 | loop fusion | flops 10649600 | bytes 656396 | tf_op jit(solution)/shard_map/convert_element_type | solution.py:457
  5.4 3.5 %collective-permute-start.1 = (bf16[1,1,32,640]{3,2,1,0:T(8,128)(2,1)S(1)}, bf16[1,1,32,640]{3,2,1,0:T(8,128)(2,1)S(1)}, u32[]{:S(2)}, u32[]{:S(2)}) collective-permute-start(bf16[1,1,32,640]{3,2,1,0:T(8,128)(2,1)S(1)} %get-tuple-element.15), channel_id=1, source_target_pairs={{8,0},{16,8},{24,16},{32,24},{40,32},{48,40},{56,48},{64,56},{72,6... | collective-permute-start | bytes 122888 | tf_op jit(solution)/shard_map/ppermute | solution.py:33
  8.9 3.1 %collective-permute-start = (bf16[1,1,32,640]{3,2,1,0:T(8,128)(2,1)S(1)}, bf16[1,1,32,640]{3,2,1,0:T(8,128)(2,1)S(1)}, u32[]{:S(2)}, u32[]{:S(2)}) collective-permute-start(bf16[1,1,32,640]{3,2,1,0:T(8,128)(2,1)S(1)} %get-tuple-element.14), channel_id=1, source_target_pairs={{0,8},{8,16},{16,24},{24,32},{32,40},{40,48},{48,56},{56,64},{64,7... | collective-permute-start | bytes 122888 | tf_op jit(solution)/shard_map/ppermute | solution.py:31
  12.1 0.9 collective-permute-done
  13.1 1.3 %collective-permute-start.3 = (bf16[1,10,1,640]{3,2,1,0:T(2,128)(2,1)S(1)}, bf16[1,10,1,640]{3,2,1,0:T(2,128)(2,1)S(1)}, u32[]{:S(2)}, u32[]{:S(2)}) collective-permute-start(bf16[1,10,1,640]{3,2,1,0:T(2,128)(2,1)S(1)} %get-tuple-element.10), channel_id=1, source_target_pairs={{1,0},{2,1},{3,2},{4,3},{5,4},{6,5},{7,6},{9,8},{10,9},{11,10},{12... | collective-permute-start | bytes 38408 | tf_op jit(solution)/shard_map/ppermute | solution.py:33
  14.4 5.5 %collective-permute-start.2 = (bf16[1,10,1,640]{3,2,1,0:T(2,128)(2,1)S(1)}, bf16[1,10,1,640]{3,2,1,0:T(2,128)(2,1)S(1)}, u32[]{:S(2)}, u32[]{:S(2)}) collective-permute-start(bf16[1,10,1,640]{3,2,1,0:T(2,128)(2,1)S(1)} %get-tuple-element.11), channel_id=1, source_target_pairs={{0,1},{1,2},{2,3},{3,4},{4,5},{5,6},{6,7},{8,9},{9,10},{10,11},{11... | collective-permute-start | bytes 38408 | tf_op jit(solution)/shard_map/ppermute | solution.py:31
  19.9 0.2 convolution_reduce_fusion
  20.1 0.7 collective-permute-done.2
  20.8 0.2 pad_maximum_fusion.1
  21.3 1.5 %constant_dynamic-update-slice_fusion = bf16[1,8,32,5760]{3,2,1,0:T(8,128)(2,1)S(1)} fusion(bf16[1,8,32,5760]{3,2,1,0:T(8,128)(2,1)S(1)} %slice_dynamic-update-slice_fusion.9, f32[]{:T(128)} %bitcast.3, s32[]{:T(128)S(6)} %xor.200, s32[8,32]{1,0:T(8,128)S(1)} %add_multiply_fusion, bf16[1,8,32,640]{3,2,1,0:T(8,128)(2,1)S(1)} %copy-done.1, f32[]{:T(128)} %bitcast), kind=kLoop, calls=%fused_computation.78 | loop fusion | flops 10649600 | bytes 659468
  22.8 0.1 slice_dynamic-update-slice_fusion.8
  23.1 0.8 copy-done.2
  23.9 2.5 %fusion.50 = bf16[1,8,32,640]{3,2,1,0:T(8,128)(2,1)S(1)} fusion(bf16[5760,640]{1,0:T(8,128)(2,1)S(1)} %copy-done.2, bf16[1,8,32,5760]{3,2,1,0:T(8,128)(2,1)S(1)} %slice_dynamic-update-slice_fusion.6, f32[640]{0:T(1024)S(1)} %convolution_reduce_fusion), kind=kOutput, calls=%fused_computation.52 | convolution fusion | flops 1888419840 | bytes 10652160 | tf_op jit(solution)/shard_map/dot_general | solution.py:464
  26.5 2.1 %collective-permute-start.5 = (bf16[1,1,32,640]{3,2,1,0:T(8,128)(2,1)S(1)}, bf16[1,1,32,640]{3,2,1,0:T(8,128)(2,1)S(1)}, u32[]{:S(2)}, u32[]{:S(2)}) collective-permute-start(bf16[1,1,32,640]{3,2,1,0:T(8,128)(2,1)S(1)} %get-tuple-element.13), channel_id=1, source_target_pairs={{8,0},{16,8},{24,16},{32,24},{40,32},{48,40},{56,48},{64,56},{72,6... | collective-permute-start | bytes 122888 | tf_op jit(solution)/shard_map/ppermute | solution.py:33
  28.6 5.2 %collective-permute-start.4 = (bf16[1,1,32,640]{3,2,1,0:T(8,128)(2,1)S(1)}, bf16[1,1,32,640]{3,2,1,0:T(8,128)(2,1)S(1)}, u32[]{:S(2)}, u32[]{:S(2)}) collective-permute-start(bf16[1,1,32,640]{3,2,1,0:T(8,128)(2,1)S(1)} %get-tuple-element.12), channel_id=1, source_target_pairs={{0,8},{8,16},{16,24},{24,32},{32,40},{40,48},{48,56},{56,64},{64,7... | collective-permute-start | bytes 122888 | tf_op jit(solution)/shard_map/ppermute | solution.py:31
  33.8 1.1 collective-permute-done.4
  34.9 1.3 %collective-permute-start.7 = (bf16[1,10,1,640]{3,2,1,0:T(2,128)(2,1)S(1)}, bf16[1,10,1,640]{3,2,1,0:T(2,128)(2,1)S(1)}, u32[]{:S(2)}, u32[]{:S(2)}) collective-permute-start(bf16[1,10,1,640]{3,2,1,0:T(2,128)(2,1)S(1)} %get-tuple-element.6), channel_id=1, source_target_pairs={{1,0},{2,1},{3,2},{4,3},{5,4},{6,5},{7,6},{9,8},{10,9},{11,10},{12... | collective-permute-start | bytes 38408 | tf_op jit(solution)/shard_map/ppermute | solution.py:33
  36.2 6.3 %collective-permute-start.6 = (bf16[1,10,1,640]{3,2,1,0:T(2,128)(2,1)S(1)}, bf16[1,10,1,640]{3,2,1,0:T(2,128)(2,1)S(1)}, u32[]{:S(2)}, u32[]{:S(2)}) collective-permute-start(bf16[1,10,1,640]{3,2,1,0:T(2,128)(2,1)S(1)} %get-tuple-element.7), channel_id=1, source_target_pairs={{0,1},{1,2},{2,3},{3,4},{4,5},{5,6},{6,7},{8,9},{9,10},{10,11},{11... | collective-permute-start | bytes 38408 | tf_op jit(solution)/shard_map/ppermute | solution.py:31
  43.2 0.3 collective-permute-done.6
  43.5 0.2 pad_maximum_fusion.2
  44.5 4.5 %multiply_convert_fusion = (bf16[1,8,32,640]{3,2,1,0:T(8,128)(2,1)}, bf16[1,8,32,640]{3,2,1,0:T(8,128)(2,1)}) fusion(s32[]{:T(128)S(6)} %xor.200, s32[8,32]{1,0:T(8,128)S(1)} %add_multiply_fusion, bf16[5760,640]{1,0:T(8,128)(2,1)S(1)} %bitcast.54, bf16[1,8,32,5760]{3,2,1,0:T(8,128)(2,1)S(1)} %slice_dynamic-update-slice_fusion, f32[]{:T(128)} %bitcast.3, ...), kind=kOutput, calls=%fused_computation.50 | convolution fusion | flops 1898250240 | bytes 11305996 | tf_op jit(solution)/shard_map/dot_general | solution.py:470
  49.0 1.2 pad_maximum_fusion.hid_ref
  50.3 72.2 %shard_map.95 = f32[1,1024]{1,0:T(1,128)} custom-call(s32[1]{0:T(128)S(6)} %xor.215.salt_ref, bf16[256,640]{1,0:T(8,128)(2,1)} %bitcast.52, bf16[3,10,32,640]{3,2,1,0:T(8,128)(2,1)} %pad_maximum_fusion.hid_ref), custom_call_target="tpu_custom_call" | custom-call | tf_op jit(solution)/shard_map/pallas_call | solution.py:387
  122.5 1.3 %copy.31 = f32[1,1024]{1,0:T(1,128)} copy(f32[1,1024]{1,0:T(1,128)} %shard_map.95) | data formatting | bytes 8192
  (42 shorter events, 1.5 us)
Async XLA Ops:
  0.6 19.3 %copy-start = (bf16[640,640]{1,0:T(8,128)(2,1)S(1)}, bf16[640,640]{1,0:T(8,128)(2,1)}, u32[]{:S(2)}) copy-start(bf16[640,640]{1,0:T(8,128)(2,1)} %param.13) | copy-start | bytes 2457604
  5.4 15.9 %copy-start.1 = (bf16[1,8,32,640]{3,2,1,0:T(8,128)(2,1)S(1)}, bf16[1,8,32,640]{3,2,1,0:T(8,128)(2,1)}, u32[]{:S(2)}) copy-start(bf16[1,8,32,640]{3,2,1,0:T(8,128)(2,1)} %param.8) | copy-start | bytes 983044
  5.4 6.7 %collective-permute-start.1 = (bf16[1,1,32,640]{3,2,1,0:T(8,128)(2,1)S(1)}, bf16[1,1,32,640]{3,2,1,0:T(8,128)(2,1)S(1)}, u32[]{:S(2)}, u32[]{:S(2)}) collective-permute-start(bf16[1,1,32,640]{3,2,1,0:T(8,128)(2,1)S(1)} %get-tuple-element.15), channel_id=1, source_target_pairs={{8,0},{16,8},{24,16},{32,24},{40,32},{48,40},{56,48},{64,56},{72,6... | collective-permute-start | bytes 122888 | tf_op jit(solution)/shard_map/ppermute | solution.py:33
  8.9 4.2 %collective-permute-start = (bf16[1,1,32,640]{3,2,1,0:T(8,128)(2,1)S(1)}, bf16[1,1,32,640]{3,2,1,0:T(8,128)(2,1)S(1)}, u32[]{:S(2)}, u32[]{:S(2)}) collective-permute-start(bf16[1,1,32,640]{3,2,1,0:T(8,128)(2,1)S(1)} %get-tuple-element.14), channel_id=1, source_target_pairs={{0,8},{8,16},{16,24},{24,32},{32,40},{40,48},{48,56},{56,64},{64,7... | collective-permute-start | bytes 122888 | tf_op jit(solution)/shard_map/ppermute | solution.py:31
  13.1 7.0 %collective-permute-start.3 = (bf16[1,10,1,640]{3,2,1,0:T(2,128)(2,1)S(1)}, bf16[1,10,1,640]{3,2,1,0:T(2,128)(2,1)S(1)}, u32[]{:S(2)}, u32[]{:S(2)}) collective-permute-start(bf16[1,10,1,640]{3,2,1,0:T(2,128)(2,1)S(1)} %get-tuple-element.10), channel_id=1, source_target_pairs={{1,0},{2,1},{3,2},{4,3},{5,4},{6,5},{7,6},{9,8},{10,9},{11,10},{12... | collective-permute-start | bytes 38408 | tf_op jit(solution)/shard_map/ppermute | solution.py:33
  14.4 6.4 %collective-permute-start.2 = (bf16[1,10,1,640]{3,2,1,0:T(2,128)(2,1)S(1)}, bf16[1,10,1,640]{3,2,1,0:T(2,128)(2,1)S(1)}, u32[]{:S(2)}, u32[]{:S(2)}) collective-permute-start(bf16[1,10,1,640]{3,2,1,0:T(2,128)(2,1)S(1)} %get-tuple-element.11), channel_id=1, source_target_pairs={{0,1},{1,2},{2,3},{3,4},{4,5},{5,6},{6,7},{8,9},{9,10},{10,11},{11... | collective-permute-start | bytes 38408 | tf_op jit(solution)/shard_map/ppermute | solution.py:31
  20.8 3.1 %copy-start.2 = (bf16[5760,640]{1,0:T(8,128)(2,1)S(1)}, bf16[5760,640]{1,0:T(8,128)(2,1)}, u32[]{:S(2)}) copy-start(bf16[5760,640]{1,0:T(8,128)(2,1)} %param.14) | copy-start | bytes 22118404
  23.0 21.5 %slice-start = ((s8[7372800]{0:T(1024)(128)(4,1)}), s8[4194304]{0:T(1024)(128)(4,1)S(1)}, s32[]{:S(2)}) async-start(s8[7372800]{0:T(1024)(128)(4,1)} %bitcast.53), calls=%async_computation | async-start | bytes 8388608
  23.9 20.6 %slice-start.1 = ((s8[7372800]{0:T(1024)(128)(4,1)}), s8[3178496]{0:T(1024)(128)(4,1)S(1)}, s32[]{:S(2)}) async-start(s8[7372800]{0:T(1024)(128)(4,1)} %bitcast.53), calls=%async_computation.1 | async-start | bytes 6356992
  26.5 7.3 %collective-permute-start.5 = (bf16[1,1,32,640]{3,2,1,0:T(8,128)(2,1)S(1)}, bf16[1,1,32,640]{3,2,1,0:T(8,128)(2,1)S(1)}, u32[]{:S(2)}, u32[]{:S(2)}) collective-permute-start(bf16[1,1,32,640]{3,2,1,0:T(8,128)(2,1)S(1)} %get-tuple-element.13), channel_id=1, source_target_pairs={{8,0},{16,8},{24,16},{32,24},{40,32},{48,40},{56,48},{64,56},{72,6... | collective-permute-start | bytes 122888 | tf_op jit(solution)/shard_map/ppermute | solution.py:33
  28.6 6.2 %collective-permute-start.4 = (bf16[1,1,32,640]{3,2,1,0:T(8,128)(2,1)S(1)}, bf16[1,1,32,640]{3,2,1,0:T(8,128)(2,1)S(1)}, u32[]{:S(2)}, u32[]{:S(2)}) collective-permute-start(bf16[1,1,32,640]{3,2,1,0:T(8,128)(2,1)S(1)} %get-tuple-element.12), channel_id=1, source_target_pairs={{0,8},{8,16},{16,24},{24,32},{32,40},{40,48},{48,56},{56,64},{64,7... | collective-permute-start | bytes 122888 | tf_op jit(solution)/shard_map/ppermute | solution.py:31
  34.9 8.3 %collective-permute-start.7 = (bf16[1,10,1,640]{3,2,1,0:T(2,128)(2,1)S(1)}, bf16[1,10,1,640]{3,2,1,0:T(2,128)(2,1)S(1)}, u32[]{:S(2)}, u32[]{:S(2)}) collective-permute-start(bf16[1,10,1,640]{3,2,1,0:T(2,128)(2,1)S(1)} %get-tuple-element.6), channel_id=1, source_target_pairs={{1,0},{2,1},{3,2},{4,3},{5,4},{6,5},{7,6},{9,8},{10,9},{11,10},{12... | collective-permute-start | bytes 38408 | tf_op jit(solution)/shard_map/ppermute | solution.py:33
  36.2 7.3 %collective-permute-start.6 = (bf16[1,10,1,640]{3,2,1,0:T(2,128)(2,1)S(1)}, bf16[1,10,1,640]{3,2,1,0:T(2,128)(2,1)S(1)}, u32[]{:S(2)}, u32[]{:S(2)}) collective-permute-start(bf16[1,10,1,640]{3,2,1,0:T(2,128)(2,1)S(1)} %get-tuple-element.7), channel_id=1, source_target_pairs={{0,1},{1,2},{2,3},{3,4},{4,5},{5,6},{6,7},{8,9},{9,10},{10,11},{11... | collective-permute-start | bytes 38408 | tf_op jit(solution)/shard_map/ppermute | solution.py:31

commit v3 on v2

--- a/solution.py
+++ b/solution.py
@@ -9,7 +9,7 @@
 from jax.sharding import PartitionSpec as P
 
 K = 1024
-FILLS = (8, 16, 36, 10, 18)
+FILLS = (12, 12, 4, 8, 24, 8, 14)
 M1 = 2146121005
 M2 = -2073254261
 MESH = pl.DeviceIdType.MESH
@@ -18,23 +18,6 @@
 def wrap32(value):
     value &= 0xFFFFFFFF
     return value - (1 << 32) if value >= (1 << 31) else value
-
-
-def extended(cells, sides, width):
-    for axis, dim in sides:
-        count = lax.axis_size(axis)
-        ends = count - 1
-        head = lax.slice_in_dim(cells, 0, width, axis=dim)
-        tail = lax.slice_in_dim(cells, cells.shape[dim] - width, cells.shape[dim], axis=dim)
-        cells = jnp.concatenate(
-            [
-                lax.ppermute(tail, axis, [(i, (i + 1) % count) for i in range(ends)]),
-                cells,
-                lax.ppermute(head, axis, [((i + 1) % count, i) for i in range(ends)]),
-            ],
-            axis=dim,
-        )
-    return cells
 
 
 def mix_bits(value):
@@ -46,39 +29,11 @@
     return value
 
 
-def noise_field(
-    example_ids, noise_seed, row_first, col_first, tile_rows, tile_cols, channels, rows_all, cols_all
-):
-    row_ids = row_first + jnp.arange(tile_rows, dtype=jnp.int32)
-    col_ids = col_first + jnp.arange(tile_cols, dtype=jnp.int32)
-    chan_ids = jnp.arange(channels, dtype=jnp.int32)
-    base = (
-        (example_ids[:, None, None, None] * rows_all + row_ids[None, :, None, None]) * cols_all
-        + col_ids[None, None, :, None]
-    ) * channels + chan_ids
-    salt = mix_bits(noise_seed[0])
-    total = jnp.zeros(base.shape, jnp.float32)
-    for salt_index in range(4):
-        bits = mix_bits(base * 4 + salt_index + salt)
-        total = total + lax.shift_right_logical(bits, jnp.int32(8)).astype(jnp.float32) * (
-            1.0 / 16777216.0
-        )
-    return (total - 2.0) * math.sqrt(3.0)
-
-
-def plan(timestep):
-    fraction = timestep.astype(jnp.float32) / 1000.0
-    return jnp.cos((fraction + 0.008) / 1.008 * (math.pi / 2.0)) ** 2
-
-
-def time_features(timestep, channels):
-    half = channels // 2
-    freqs = jnp.exp(-math.log(10000.0) * jnp.arange(half, dtype=jnp.float32) / half)
-    angles = timestep.astype(jnp.float32)[:, None] * freqs[None, :]
-    return jnp.concatenate([jnp.sin(angles), jnp.cos(angles)], axis=1)
-
-
 CH = 640
+ROWS = 128
+COLS = 256
+TH = 8
+TW = 32
 TAPS = 9 * CH
 THIRD = 3 * CH
 CUT = 1024
@@ -122,6 +77,29 @@
         for step in range(1, 4):
             out.append(device(at, **{axis: hop(at, axis, step)}))
     return out
+
+
+def silu(value):
+    return value / (1.0 + jnp.exp(-value))
+
+
+def rounded(value):
+    return value.astype(jnp.bfloat16)
+
+
+def field(rows, cols, example, salt):
+    lane = lax.broadcasted_iota(jnp.int32, (1, CH), 1)
+    base = ((example * ROWS + rows) * COLS + cols) * (4 * CH) + salt
+    base = base + lane * 4
+    total = None
+    for index in range(4):
+        bits = shift_right(mix_bits(base + index), 8)
+        total = bits if total is None else total + bits
+    return (f32(total) * (1.0 / 16777216.0) - 2.0) * math.sqrt(3.0)
+
+
+def inside(rows, cols):
+    return (rows >= 0) & (rows < ROWS) & (cols >= 0) & (cols < COLS)
 
 
 def selection(third, core):
@@ -208,18 +186,95 @@
     return pltpu.roll(jnp.where(j >= s, total[0:1], total[1:2]), (K - s) & (K - 1), axis=1)
 
 
-def back_kernel(
-    salt_ref, cot_ref, hid_ref, out_ref,
-    cot_far, hid_far, lhs, s1, r1a, r1b, r1, f2, s2, r2a, r2b, r2, f3, r3, row, grow, acc, bits,
+def kernel(
+    step_ref, noise_seed_ref, proj_seed_ref, example_ref, latent_ref, time_ref, w1_ref, w2_ref,
+    section_ref, out_ref,
+    stage, tall, side_in, corner_in, weight, actx, side_lhs, noise_keep, noisy_keep,
+    hid_near, hid_far, cot_near, cot_far,
+    lhs, s1, r1a, r1b, r1, s2, r2a, r2b, r2, f3, r3, row, grow, acc, bits,
     sum8, sum4, sum4b,
+    load_sem, rim_send, rim_recv,
     pair_send, pair_recv, ring_send, ring_recv, tail_send, tail_recv, all_send, all_recv,
 ):
     at = place()
+    r_index = lax.axis_index("row")
+    c_index = lax.axis_index("col")
     peers = peers_of(at)
+    around = []
+    for dr in (-1, 0, 1):
+        for dc in (-1, 0, 1):
+            if dr or dc:
+                around.append((dr, dc))
+
+    def beside(dr, dc):
+        return (lax.rem(r_index + (16 + dr), 16), lax.rem(c_index + (8 + dc), 8))
+
     barrier = pltpu.get_barrier_semaphore()
-    for peer in peers:
+    greeted = peers + [beside(dr, dc) for dr, dc in around]
+    for peer in greeted:
         pl.semaphore_signal(barrier, inc=1, device_id=peer, device_id_type=MESH)
-    pl.semaphore_wait(barrier, len(peers))
+
+    def load(source, part):
+        rows = pl.ds(part * THIRD, THIRD)
+        return pltpu.make_async_copy(source.at[rows], weight.at[rows], load_sem.at[part])
+
+    for part in range(3):
+        load(w1_ref, part).start()
+
+    salt = mix_bits(proj_seed_ref[0] + jnp.int32(12345))
+    owner = ((at["core"] * 4 + at["x"]) * 4 + at["y"]) * 4 + at["z"]
+    marks = [0]
+
+    def fill(count):
+        low = marks[-1]
+        high = min(low + count, PADDED // 256)
+        marks.append(high)
+        if high > low:
+            make_signs(salt, owner * RUN, bits, low, high)
+
+    def pack(cells):
+        rows = [f32(latent_ref[0, r])[c : c + 1] for r, c in cells]
+        if len(rows) < 16:
+            rows.append(jnp.zeros((16 - len(rows), CH), jnp.float32))
+        return rounded(jnp.concatenate(rows, axis=0))
+
+    edge = {-1: (0, 1), 1: (TW - 2, TW - 1)}
+    brim = {-1: (0, 1), 1: (TH - 2, TH - 1)}
+    for index, dc in enumerate((-1, 1)):
+        stage[index] = pack([(r, c) for c in edge[dc] for r in range(TH)])
+        for other, dr in enumerate((-1, 1)):
+            stage[2 + other * 2 + index] = pack([(r, c) for c in edge[dc] for r in brim[dr]])
+
+    example = example_ref[0]
+    noise_salt = mix_bits(noise_seed_ref[0])
+    row_first = r_index * TH
+    col_first = c_index * TW
+    when = jnp.broadcast_to(step_ref[0], (1, CH)).astype(jnp.float32)
+    abar = jnp.cos((when / 1000.0 + 0.008) / 1.008 * (math.pi / 2.0)) ** 2
+    keep = jnp.sqrt(abar)
+    spoil = jnp.sqrt(1.0 - abar)
+    col_here = lax.broadcasted_iota(jnp.int32, (TW, 1), 0)
+
+    def noised(latent, rows, cols):
+        noise = field(rows, cols, example, noise_salt)
+        noisy = rounded(keep * f32(latent) + spoil * noise)
+        act = f32(rounded(silu(f32(noisy))))
+        return noise, noisy, act
+
+    def middle(r):
+        latent = latent_ref[0, r]
+        noise, noisy, act = noised(latent, col_here * 0 + (row_first + r), col_first + col_here)
+        noise_keep[r] = noise
+        noisy_keep[r] = noisy
+        actx[r + 2, :, CH : 2 * CH] = rounded(act)
+
+    def middles(r, carry):
+        middle(r)
+        return carry
+
+    lax.fori_loop(0, TH, middles, 0)
+    fill(FILLS[0])
+    pl.semaphore_wait(barrier, len(greeted))
 
     def send(src, dst, send_sem, recv_sem, to):
         copy = pltpu.make_async_remote_copy(
@@ -229,31 +284,133 @@
         copy.start()
         return copy
 
-    salt = salt_ref[0]
-    owner = ((at["core"] * 4 + at["x"]) * 4 + at["y"]) * 4 + at["z"]
-    marks = [0]
-
-    def fill(count):
-        low = marks[-1]
-        high = min(low + count, PADDED // 256)
-        marks.append(high)
-        if high > low:
-            make_signs(salt, owner * RUN, bits, low, high)
+    rims = []
+    for index, (dr, dc) in enumerate(around):
+        if dc == 0:
+            src = latent_ref.at[0, pl.ds(brim[dr][0], 2)]
+            dst = tall.at[0 if dr > 0 else 1]
+        elif dr == 0:
+            src = stage.at[0 if dc < 0 else 1]
+            dst = side_in.at[0 if dc > 0 else 1]
+        else:
+            src = stage.at[2 + (0 if dr < 0 else 2) + (0 if dc < 0 else 1)]
+            dst = corner_in.at[(0 if dr > 0 else 2) + (0 if dc > 0 else 1)]
+        rims.append(send(src, dst, rim_send.at[index], rim_recv.at[index], beside(dr, dc)))
+    started = list(rims)
+
+    lane = lax.broadcasted_iota(jnp.int32, (1, CH), 1)
+    half = jnp.where(lane < CH // 2, lane, lane - CH // 2)
+    angle = when * jnp.exp(f32(half) * (-math.log(10000.0)) / (CH // 2))
+    wave = jnp.where(lane < CH // 2, jnp.sin(angle), jnp.cos(angle))
+    wave = rounded(jnp.concatenate([wave, jnp.zeros((15, CH), jnp.float32)], axis=0))
+    temb = jnp.dot(wave, time_ref[...], preferred_element_type=jnp.float32)[0:1]
+    fill(FILLS[1])
+    for copy in rims:
+        copy.wait_recv()
+
+    def outer(which, r, grid_row):
+        rows = col_here * 0 + grid_row
+        cols = col_first + col_here
+        act = noised(tall[which, r], rows, cols)[2]
+        return jnp.where(inside(rows, cols), act, 0.0)
+
+    for which, first in ((0, -2), (1, TH)):
+        for r in range(2):
+            act = outer(which, r, row_first + (first + r))
+            actx[first + 2 + r, :, CH : 2 * CH] = rounded(act)
+    flank = lax.broadcasted_iota(jnp.int32, (16, 1), 0)
+    sides = []
+    for index, first in enumerate((-2, TW)):
+        rows = row_first + (flank & 7)
+        cols = col_first + first + shift_right(flank, 3)
+        act = noised(side_in[index], rows, cols)[2]
+        sides.append(jnp.where(inside(rows, cols), act, 0.0))
+    corners = jnp.concatenate([f32(corner_in[index])[0:4] for index in range(4)], axis=0)
+    kind = shift_right(flank, 2)
+    rows = row_first + (flank & 1) + jnp.where(kind < 2, -2, TH)
+    cols = col_first + (shift_right(flank, 1) & 1) + jnp.where((kind & 1) == 0, -2, TW)
+    corners = jnp.where(inside(rows, cols), noised(corners, rows, cols)[2], 0.0)
+
+    def column(side, which):
+        top = corners[4 * side + 2 * which : 4 * side + 2 * which + 2]
+        bottom = corners[8 + 4 * side + 2 * which : 8 + 4 * side + 2 * which + 2]
+        return jnp.concatenate([top, sides[side][8 * which : 8 * which + 8], bottom], axis=0)
+
+    centre = [f32(actx[r, :, CH : 2 * CH]) for r in range(TH + 4)]
+    lefts = [column(0, 0), column(0, 1), jnp.concatenate([c[0:1] for c in centre], axis=0)]
+    rights = [jnp.concatenate([c[TW - 1 : TW] for c in centre], axis=0), column(1, 0), column(1, 1)]
+    for r in range(TH + 4):
+        cell = centre[r]
+        actx[r, :, 0:CH] = rounded(
+            jnp.where(col_here == 0, lefts[1][r : r + 1], pltpu.roll(cell, 1, axis=0))
+        )
+        actx[r, :, 2 * CH : 3 * CH] = rounded(
+            jnp.where(col_here == TW - 1, rights[1][r : r + 1], pltpu.roll(cell, TW - 1, axis=0))
+        )
+    for dy in range(3):
+        for dx in range(3):
+            both = [lefts[dx][dy : dy + 10], rights[dx][dy : dy + 10], jnp.zeros((12, CH), jnp.float32)]
+            side_lhs[dy, :, dx * CH : (dx + 1) * CH] = rounded(jnp.concatenate(both, axis=0))
+
+    total = None
+    for dy in range(3):
+        load(w1_ref, dy).wait()
+        left = jnp.concatenate(
+            [actx[dy : dy + TH + 2].reshape((TH + 2) * TW, THIRD), side_lhs[dy]], axis=0
+        )
+        part = jnp.dot(left, weight[dy * THIRD : (dy + 1) * THIRD], preferred_element_type=jnp.float32)
+        total = part if total is None else total + part
+        load(w2_ref, dy).start()
+    hidden = silu(total + temb)
+    flanks = hidden[(TH + 2) * TW :]
+    flank = lax.broadcasted_iota(jnp.int32, (32, 1), 0)
+    right_side = jnp.where(flank < 10, 0, 1)
+    rows = row_first - 1 + flank - right_side * 10
+    cols = col_first - 1 + right_side * (TW + 1)
+    flanks = jnp.where(inside(rows, cols), flanks, 0.0)
+    for r in range(TH + 2):
+        cell = hidden[r * TW : (r + 1) * TW]
+        if r in (0, TH + 1):
+            rows = col_here * 0 + (row_first + (r - 1))
+            cell = jnp.where(inside(rows, col_first + col_here), cell, 0.0)
+        hid_near[r, :, CH : 2 * CH] = rounded(cell)
+        hid_near[r, :, 0:CH] = rounded(
+            jnp.where(col_here == 0, flanks[r : r + 1], pltpu.roll(cell, 1, axis=0))
+        )
+        hid_near[r, :, 2 * CH : 3 * CH] = rounded(
+            jnp.where(col_here == TW - 1, flanks[10 + r : 11 + r], pltpu.roll(cell, TW - 1, axis=0))
+        )
 
     partner = device(at, core=lax.rem(at["core"] + 1, 2))
-    pair = [
-        send(cot_ref, cot_far, pair_send.at[0], pair_recv.at[0], partner),
-        send(hid_ref, hid_far, pair_send.at[1], pair_recv.at[1], partner),
-    ]
-    fill(FILLS[0])
-    pair[0].wait_recv()
-    for third in range(3):
-        pick = selection(third, at["core"])
-        for side, cot in enumerate((cot_ref, cot_far)):
+    pair = [send(hid_near, hid_far, pair_send.at[1], pair_recv.at[1], partner)]
+    fill(FILLS[2])
+
+    total = None
+    for dy in range(3):
+        load(w2_ref, dy).wait()
+        part = jnp.dot(
+            hid_near[dy : dy + TH].reshape(TH * TW, THIRD), weight[dy * THIRD : (dy + 1) * THIRD],
+            preferred_element_type=jnp.float32,
+        )
+        total = part if total is None else total + part
+    for r in range(TH):
+        full = f32(noisy_keep[r]) + total[r * TW : (r + 1) * TW]
+        section_ref[0, r] = rounded(full)
+        cot_near[r * TW : (r + 1) * TW] = rounded((full - noise_keep[r]) * (1.0 / math.sqrt(ROWS * COLS)))
+    pair.append(send(cot_near, cot_far, pair_send.at[0], pair_recv.at[0], partner))
+    started += pair
+    picks = [selection(third, at["core"]) for third in range(3)]
+
+    def gather(side, cot):
+        for third in range(3):
             lhs[third, side] = lax.dot_general(
-                pick, cot[...], (((1,), (1,)), ((), ())), preferred_element_type=jnp.float32
+                picks[third], cot[...], (((1,), (1,)), ((), ())), preferred_element_type=jnp.float32
             ).astype(jnp.bfloat16)
-    pair[1].wait_recv()
+
+    gather(0, cot_near)
+    for copy in pair:
+        copy.wait_recv()
+    gather(1, cot_far)
 
     def ring_one(third, level, blocks, ra, rb):
         axis = ORDERS[third][level]
@@ -287,20 +444,18 @@
                     device(at, **{axis: below}))
         return [up, down]
 
-    started = list(pair)
     ones = []
     for third in range(3):
-        for dx in range(3):
-            near = hid_ref[dx, third : third + 8].reshape(256, CH)
-            far = hid_far[dx, third : third + 8].reshape(256, CH)
-            total = jnp.dot(lhs[third, 0], near, preferred_element_type=jnp.float32)
-            total += jnp.dot(lhs[third, 1], far, preferred_element_type=jnp.float32)
-            s1[third, :, :, dx * CH : (dx + 1) * CH] = total.astype(jnp.bfloat16).reshape(4, 80, CH)
+        near = hid_near[third : third + TH].reshape(TH * TW, THIRD)
+        far = hid_far[third : third + TH].reshape(TH * TW, THIRD)
+        total = jnp.dot(lhs[third, 0], near, preferred_element_type=jnp.float32)
+        total += jnp.dot(lhs[third, 1], far, preferred_element_type=jnp.float32)
+        s1[third] = rounded(total).reshape(4, 80, THIRD)
         ones.append(ring_one(third, 0, s1, r1a, r1b))
-    fill(FILLS[1])
+    fill(FILLS[3])
     twos = [ring_two(t, 0, s1, r1a, r1b, ones[t], r1) for t in range(3)]
     started += [copy for group in ones + twos for copy in group]
-    fill(FILLS[2])
+    fill(FILLS[4])
     ones = []
     for third in range(3):
         mine = at[ORDERS[third][0]]
@@ -309,21 +464,20 @@
         total = f32(s1[third, mine]) + f32(r1[third, 0]) + f32(r1[third, 1])
         for block in range(4):
             piece = total[block * 20 : block * 20 + 20]
-            f2[third, block, 0:20] = piece
             s2[third, block] = jnp.concatenate([piece, jnp.zeros((12, THIRD), jnp.float32)], axis=0).astype(
                 jnp.bfloat16
             )
         ones.append(ring_one(third, 1, s2, r2a, r2b))
-    fill(FILLS[3])
+    fill(FILLS[5])
     twos = [ring_two(t, 1, s2, r2a, r2b, ones[t], r2) for t in range(3)]
     started += [copy for group in ones + twos for copy in group]
-    fill(FILLS[4])
+    fill(FILLS[6])
     lasts = []
     for third in range(3):
         mine = at[ORDERS[third][1]]
         for copy in twos[third]:
             copy.wait_recv()
-        total = f2[third, mine, 0:20] + f32(r2[third, 0, 0:20]) + f32(r2[third, 1, 0:20])
+        total = f32(s2[third, mine, 0:20]) + f32(r2[third, 0, 0:20]) + f32(r2[third, 1, 0:20])
         for block in range(4):
             f3[third, block] = jnp.concatenate(
                 [total[block * OWN : (block + 1) * OWN], jnp.zeros((3, THIRD), jnp.float32)], axis=0
@@ -380,28 +534,39 @@
         copy.wait_send()
 
 
-def back(salt, cot, hid):
+def call(step, noise_seed, proj_seed, example, latent, time_weight, w1, w2):
     bf16, full = jnp.bfloat16, jnp.float32
     vmem = pltpu.VMEM
     dma = pltpu.SemaphoreType.DMA
+    scalar = pl.BlockSpec(memory_space=pltpu.SMEM)
+    near = pl.BlockSpec(memory_space=pltpu.VMEM)
     return pl.pallas_call(
-        back_kernel,
-        out_shape=jax.ShapeDtypeStruct((1, K), full),
-        in_specs=[
-            pl.BlockSpec(memory_space=pltpu.SMEM),
-            pl.BlockSpec(memory_space=pltpu.VMEM),
-            pl.BlockSpec(memory_space=pltpu.VMEM),
-        ],
-        out_specs=pl.BlockSpec(memory_space=pltpu.VMEM),
+        kernel,
+        out_shape=(
+            jax.ShapeDtypeStruct(latent.shape, bf16),
+            jax.ShapeDtypeStruct((1, K), full),
+        ),
+        in_specs=[scalar] * 4 + [near] * 2 + [pl.BlockSpec(memory_space=pl.ANY)] * 2,
+        out_specs=(near, near),
         scratch_shapes=[
-            vmem((256, CH), bf16),
-            vmem((3, 10, 32, CH), bf16),
+            vmem((6, 16, CH), bf16),
+            vmem((2, 2, TW, CH), bf16),
+            vmem((2, 16, CH), bf16),
+            vmem((4, 16, CH), bf16),
+            vmem((TAPS, CH), bf16),
+            vmem((TH + 4, TW, THIRD), bf16),
+            vmem((3, 32, THIRD), bf16),
+            vmem((TH, TW, CH), full),
+            vmem((TH, TW, CH), bf16),
+            vmem((TH + 2, TW, THIRD), bf16),
+            vmem((TH + 2, TW, THIRD), bf16),
+            vmem((TH * TW, CH), bf16),
+            vmem((TH * TW, CH), bf16),
             vmem((3, 2, 320, 256), bf16),
             vmem((3, 4, 80, THIRD), bf16),
             vmem((3, 80, CUT), bf16),
             vmem((3, 80, THIRD - CUT), bf16),
             vmem((3, 2, 80, THIRD), bf16),
-            vmem((3, 4, 24, THIRD), full),
             vmem((3, 4, 32, THIRD), bf16),
             vmem((3, 32, CUT), bf16),
             vmem((3, 32, THIRD - CUT), bf16),
@@ -415,6 +580,8 @@
             vmem((8, 1, K), full),
             vmem((4, 1, K), full),
             vmem((4, 1, K), full),
+            dma((3,)),
+            dma((8,)), dma((8,)),
             dma((2,)), dma((2,)),
             dma((3, 2, 4)), dma((3, 2, 4)),
             dma((3, 3)), dma((3, 3)),
@@ -423,63 +590,15 @@
         compiler_params=pltpu.CompilerParams(
             collective_id=0, has_side_effects=True, vmem_limit_bytes=60 * 2**20
         ),
-    )(salt, cot, hid)
-
-
-def unfold(padded, tile_rows, tile_cols):
-    pieces = []
-    for row_off in range(3):
-        for col_off in range(3):
-            pieces.append(
-                padded[:, row_off : row_off + tile_rows, col_off : col_off + tile_cols, :]
-            )
-    joined = jnp.concatenate(pieces, axis=3)
-    return joined.reshape(joined.shape[0], tile_rows * tile_cols, joined.shape[3])
+    )(step, noise_seed, proj_seed, example, latent, time_weight, w1, w2)
 
 
 def on_device(
     latent, timestep, noise_seed, proj_seed, example_ids, time_weight, conv1_weight, conv2_weight
 ):
-    batch, tile_rows, tile_cols, channels = latent.shape
-    rows_count = lax.axis_size("row")
-    cols_count = lax.axis_size("col")
-    rows_all = tile_rows * rows_count
-    cols_all = tile_cols * cols_count
-    row_first = lax.axis_index("row") * tile_rows
-    col_first = lax.axis_index("col") * tile_cols
-    noise = noise_field(
-        example_ids, noise_seed, row_first, col_first, tile_rows, tile_cols, channels, rows_all, cols_all
+    return call(
+        timestep, noise_seed, proj_seed, example_ids, latent, time_weight, conv1_weight, conv2_weight
     )
-    abar = plan(timestep)[:, None, None, None]
-    noisy = (jnp.sqrt(abar) * latent.astype(jnp.float32) + jnp.sqrt(1.0 - abar) * noise).astype(
-        jnp.bfloat16
-    )
-    act = jax.nn.silu(noisy.astype(jnp.float32)).astype(jnp.bfloat16)
-    act_pad = extended(act, (("row", 1), ("col", 2)), 1)
-    features = time_features(timestep, channels).astype(jnp.bfloat16)
-    temb = jnp.dot(features, time_weight, preferred_element_type=jnp.float32)
-    act_cols = unfold(act_pad, tile_rows, tile_cols).reshape(
-        batch * tile_rows * tile_cols, 9 * channels
-    )
-    pre = jnp.dot(act_cols, conv1_weight, preferred_element_type=jnp.float32).reshape(
-        batch, tile_rows, tile_cols, channels
-    )
-    hidden = jax.nn.silu(pre + temb[:, None, None, :]).astype(jnp.bfloat16)
-    hid_pad = extended(hidden, (("row", 1), ("col", 2)), 1)
-    hid_cols = unfold(hid_pad, tile_rows, tile_cols)
-    conv_out = jnp.dot(
-        hid_cols.reshape(batch * tile_rows * tile_cols, 9 * channels),
-        conv2_weight,
-        preferred_element_type=jnp.float32,
-    )
-    out_full = noisy.astype(jnp.float32) + conv_out.reshape(batch, tile_rows, tile_cols, channels)
-    section_out = out_full.astype(jnp.bfloat16)
-    cot = ((out_full - noise) / math.sqrt(rows_all * cols_all)).astype(jnp.bfloat16)
-    cot = cot.reshape(batch * tile_rows * tile_cols, channels)
-    shifted = jnp.stack([hid_pad[0, :, dx : dx + tile_cols, :] for dx in range(3)])
-    salt = mix_bits(proj_seed + jnp.int32(12345))
-    sketch = back(salt, cot, shifted)
-    return (section_out, sketch)
 
 
 def solution(mesh):

time: 125 us -> 88.8 us (0.71)
  starting transfers between devices: 28.3 us -> 0 us
  Pallas kernels: 72.2 us -> 81.8 us
  matrix products: 7.26 us -> 0 us
  other arithmetic: 6.03 us -> 0 us
  waiting for transfers between devices: 2.97 us -> 0 us
    ppermute x8 -> x0, starting transfers between devices: 28.3 us -> none  [the longest x4 20.1 us: extended(): lax.ppermute(tail, axis, [(i, (i + 1) % count) for i in range(ends)])]
    pallas_call x1, Pallas kernels: 72.2 us -> 81.8 us  [call(): pl.pallas_call(kernel, out_shape=(jax.ShapeDtypeStruct(latent.shape, bf16...]
    dot_general x3 -> x0, matrix products: 7.26 us -> none  [the longest x1 4.51 us: on_device(): jnp.dot(hid_cols.reshape(batch * tile_rows * tile_cols, 9 * channels), co...]
    ppermute x8 -> x0, waiting for transfers between devices: 2.97 us -> none  [the longest x4 2.96 us: extended(): lax.ppermute(tail, axis, [(i, (i + 1) % count) for i in range(ends)])]
    convert_element_type x1 -> x0, other arithmetic: 2.42 us -> none  [on_device(): act = jax.nn.silu(noisy.astype(jnp.float32)).astype(jnp.bfloat16)]
    unnamed x6 -> x0, other arithmetic: 1.65 us -> none
    another operation x2 -> x0, other arithmetic: 1.28 us -> none  [the longest x1 1.23 us: on_device(): jnp.stack([hid_pad[0, :, dx:dx + tile_cols, :] for dx in range(3)])]
    unnamed x22 -> x2, local copies, waits for them, and re-layouts: 2.82 us -> 3 us
  transfers between devices with their start and end apart: 8 -> 0, of which waited for: 4 -> 0; matrix products, arithmetic and copies ran while one was open for 0% -> 0% of each run, Pallas kernels for 0% -> 0%
where the time goes in v3:
time: 88.8 us; the launch traced here: 88 us
  Pallas kernels  81.8 us (92%)
  between operations  3.22 us (4%)
  local copies, waits for them, and re-layouts  3 us (3%)
    pallas_call x1, Pallas kernels, call(): pl.pallas_call(kernel, out_shape=(jax.ShapeDtypeStruct(latent.shape, bf16...  81.8 us
    unnamed x2, local copies, waits for them, and re-layouts  3 us

profile of v3, /device:TPU:1, one launch (start us, length us, event | category | flops | bytes accessed | tf_op | source)
XLA Modules:
  0.0 88.0 jit_solution(17862787932219994910)
XLA Ops:
  3.2 81.8 %shard_map.95 = (bf16[1,8,32,640]{3,2,1,0:T(8,128)(2,1)}, f32[1,1024]{1,0:T(1,128)}) custom-call(s32[1]{0:T(128)S(6)} %copy.12.step_ref, s32[1]{0:T(128)S(6)} %copy.13.noise_seed_ref, s32[1]{0:T(128)S(6)} %copy.14.proj_seed_ref, s32[1]{0:T(128)S(6)} %copy.15.example_ref, bf16[1,8,32,640]{3,2,1,0:T(8,128)(2,1)} %latent_ref.1, bf16[640,640]{1,0:T(8,128)(2,1)} %time_ref.1, ...), custom_call_target="tpu_custom_call" | custom-call | tf_op jit(solution)/shard_map/pallas_call | solution.py:543
  85.0 1.7 %copy.16 = bf16[1,8,32,640]{3,2,1,0:T(8,128)(2,1)} copy(bf16[1,8,32,640]{3,2,1,0:T(8,128)(2,1)} %get-tuple-element.4) | data formatting | bytes 655360
  86.7 1.3 %copy.17 = f32[1,1024]{1,0:T(1,128)} copy(f32[1,1024]{1,0:T(1,128)} %get-tuple-element.5) | data formatting | bytes 8192

commit v4 on v3

--- a/solution.py
+++ b/solution.py
@@ -9,7 +9,7 @@
 from jax.sharding import PartitionSpec as P
 
 K = 1024
-FILLS = (12, 12, 4, 8, 24, 8, 14)
+FILLS = (8, 8, 0, 18, 34, 26)
 M1 = 2146121005
 M2 = -2073254261
 MESH = pl.DeviceIdType.MESH
@@ -36,6 +36,7 @@
 TW = 32
 TAPS = 9 * CH
 THIRD = 3 * CH
+TILES = THIRD // 128
 CUT = 1024
 OWN = 5
 RUN = OWN * TAPS
@@ -73,9 +74,10 @@
         for flip in range(2):
             if step or flip:
                 out.append(device(at, x=hop(at, "x", step), core=lax.rem(at["core"] + flip, 2)))
-    for axis in ("y", "z"):
-        for step in range(1, 4):
-            out.append(device(at, **{axis: hop(at, axis, step)}))
+    for up in range(4):
+        for deep in range(4):
+            if up or deep:
+                out.append(device(at, y=hop(at, "y", up), z=hop(at, "z", deep)))
     return out
 
 
@@ -187,14 +189,14 @@
 
 
 def kernel(
-    step_ref, noise_seed_ref, proj_seed_ref, example_ref, latent_ref, time_ref, w1_ref, w2_ref,
+    step_in, noise_seed_in, proj_seed_in, example_in, latent_ref, time_ref, w1_ref, w2_ref,
     section_ref, out_ref,
     stage, tall, side_in, corner_in, weight, actx, side_lhs, noise_keep, noisy_keep,
     hid_near, hid_far, cot_near, cot_far,
-    lhs, s1, r1a, r1b, r1, s2, r2a, r2b, r2, f3, r3, row, grow, acc, bits,
-    sum8, sum4, sum4b,
+    lhs, s1, r1a, r1b, r1, s2, r2, s3, r3, row, grow, acc, bits,
+    sum8, sum16, step_ref, noise_seed_ref, proj_seed_ref, example_ref, scalar_sem,
     load_sem, rim_send, rim_recv,
-    pair_send, pair_recv, ring_send, ring_recv, tail_send, tail_recv, all_send, all_recv,
+    pair_send, pair_recv, ring_send, ring_recv, two_send, two_recv, tail_send, tail_recv, all_send, all_recv,
 ):
     at = place()
     r_index = lax.axis_index("row")
@@ -218,8 +220,17 @@
         rows = pl.ds(part * THIRD, THIRD)
         return pltpu.make_async_copy(source.at[rows], weight.at[rows], load_sem.at[part])
 
+    scalars = []
+    for index, (source, held) in enumerate((
+        (step_in, step_ref), (noise_seed_in, noise_seed_ref),
+        (proj_seed_in, proj_seed_ref), (example_in, example_ref),
+    )):
+        scalars.append(pltpu.make_async_copy(source, held, scalar_sem.at[index]))
+        scalars[-1].start()
     for part in range(3):
         load(w1_ref, part).start()
+    for copy in scalars:
+        copy.wait()
 
     salt = mix_bits(proj_seed_ref[0] + jnp.int32(12345))
     owner = ((at["core"] * 4 + at["x"]) * 4 + at["y"]) * 4 + at["z"]
@@ -272,7 +283,6 @@
         middle(r)
         return carry
 
-    lax.fori_loop(0, TH, middles, 0)
     fill(FILLS[0])
     pl.semaphore_wait(barrier, len(greeted))
 
@@ -297,6 +307,8 @@
             dst = corner_in.at[(0 if dr > 0 else 2) + (0 if dc > 0 else 1)]
         rims.append(send(src, dst, rim_send.at[index], rim_recv.at[index], beside(dr, dc)))
     started = list(rims)
+
+    lax.fori_loop(0, TH, middles, 0)
 
     lane = lax.broadcasted_iota(jnp.int32, (1, CH), 1)
     half = jnp.where(lane < CH // 2, lane, lane - CH // 2)
@@ -456,79 +468,77 @@
     twos = [ring_two(t, 0, s1, r1a, r1b, ones[t], r1) for t in range(3)]
     started += [copy for group in ones + twos for copy in group]
     fill(FILLS[4])
-    ones = []
+    def spread(third, level, blocks, landed, sends, recvs):
+        axis = ORDERS[third][level]
+        group = []
+        for step in range(1, 4):
+            to = hop(at, axis, step)
+            group.append(
+                send(blocks.at[third, to], landed.at[third, step - 1],
+                     sends.at[third, step - 1], recvs.at[third, step - 1], device(at, **{axis: to}))
+            )
+        return group
+
+    def gathered(third, level, blocks, landed, group):
+        for copy in group:
+            copy.wait_recv()
+        total = f32(blocks[third, at[ORDERS[third][level]]])
+        for index in range(3):
+            total = total + f32(landed[third, index])
+        return total
+
+    seconds = []
     for third in range(3):
         mine = at[ORDERS[third][0]]
         for copy in twos[third]:
             copy.wait_recv()
         total = f32(s1[third, mine]) + f32(r1[third, 0]) + f32(r1[third, 1])
         for block in range(4):
-            piece = total[block * 20 : block * 20 + 20]
-            s2[third, block] = jnp.concatenate([piece, jnp.zeros((12, THIRD), jnp.float32)], axis=0).astype(
-                jnp.bfloat16
-            )
-        ones.append(ring_one(third, 1, s2, r2a, r2b))
+            pieces = [
+                total[block * 20 : block * 20 + 20, tile * 128 : tile * 128 + 128] for tile in range(TILES)
+            ]
+            pieces.append(jnp.zeros((4, 128), jnp.float32))
+            s2[third, block] = rounded(jnp.concatenate(pieces, axis=0))
+        seconds.append(spread(third, 1, s2, r2, two_send, two_recv))
     fill(FILLS[5])
-    twos = [ring_two(t, 1, s2, r2a, r2b, ones[t], r2) for t in range(3)]
-    started += [copy for group in ones + twos for copy in group]
-    fill(FILLS[6])
-    lasts = []
+    thirds = []
     for third in range(3):
-        mine = at[ORDERS[third][1]]
-        for copy in twos[third]:
-            copy.wait_recv()
-        total = f32(s2[third, mine, 0:20]) + f32(r2[third, 0, 0:20]) + f32(r2[third, 1, 0:20])
+        total = gathered(third, 1, s2, r2, seconds[third])
         for block in range(4):
-            f3[third, block] = jnp.concatenate(
-                [total[block * OWN : (block + 1) * OWN], jnp.zeros((3, THIRD), jnp.float32)], axis=0
-            )
-        axis = ORDERS[third][2]
-        group = []
-        for step in range(1, 4):
-            to = hop(at, axis, step)
-            group.append(
-                send(f3.at[third, to], r3.at[third, step - 1],
-                     tail_send.at[third, step - 1], tail_recv.at[third, step - 1],
-                     device(at, **{axis: to}))
-            )
-        lasts.append(group)
+            pieces = []
+            for tile in range(TILES):
+                first = tile * 20 + block * OWN
+                pieces.append(total[first : first + OWN])
+            pieces.append(jnp.zeros((5, 128), jnp.float32))
+            s3[third, block] = rounded(jnp.concatenate(pieces, axis=0))
+        thirds.append(spread(third, 2, s3, r3, tail_send, tail_recv))
+    started += [copy for group in seconds + thirds for copy in group]
     fill(PADDED)
     row[...] = jnp.zeros_like(row)
     for third in range(3):
-        mine = at[ORDERS[third][2]]
-        for copy in lasts[third]:
-            copy.wait_recv()
-        started += lasts[third]
-        total = f3[third, mine] + r3[third, 0] + r3[third, 1] + r3[third, 2]
-        for channel in range(OWN):
-            lanes = pl.ds(channel * TAPS + third * THIRD, THIRD)
-            row[0:1, lanes] = total[channel : channel + 1]
+        total = gathered(third, 2, s3, r3, thirds[third])
+        for tile in range(TILES):
+            for channel in range(OWN):
+                lanes = pl.ds(channel * TAPS + third * THIRD + tile * 128, 128)
+                row[0:1, lanes] = total[tile * OWN + channel : tile * OWN + channel + 1]
 
     share = project(salt, owner * RUN, row, grow, bits, acc)
 
     share = share * (1.0 / math.sqrt(9.0 * CH * CH))
-    me = at["x"] * 2 + at["core"]
-    sum8[me] = share
-    group = []
-    for index, peer in enumerate(peers[:7]):
-        group.append(send(sum8.at[me], sum8.at[me], all_send.at[index], all_recv.at[index], peer))
-    for copy in group:
-        copy.wait_recv()
-    started += group
-    share = sum8[0]
-    for index in range(1, 8):
-        share = share + sum8[index]
-    for axis, slots, base in (("y", sum4, 7), ("z", sum4b, 10)):
-        me = at[axis]
+    for slots, me, first, count in (
+        (sum8, at["x"] * 2 + at["core"], 0, 7),
+        (sum16, at["y"] * 4 + at["z"], 7, 15),
+    ):
         slots[me] = share
         group = []
-        for index in range(3):
-            group.append(send(slots.at[me], slots.at[me], all_send.at[base + index],
-                              all_recv.at[base + index], peers[base + index]))
+        for index in range(first, first + count):
+            group.append(send(slots.at[me], slots.at[me], all_send.at[index], all_recv.at[index], peers[index]))
         for copy in group:
             copy.wait_recv()
         started += group
-        share = slots[0] + slots[1] + slots[2] + slots[3]
+        share = slots[0]
+        for index in range(1, count + 1):
+            share = share + slots[index]
     out_ref[...] = share
     for copy in started:
         copy.wait_send()
@@ -538,7 +548,7 @@
     bf16, full = jnp.bfloat16, jnp.float32
     vmem = pltpu.VMEM
     dma = pltpu.SemaphoreType.DMA
-    scalar = pl.BlockSpec(memory_space=pltpu.SMEM)
+    scalar = pl.BlockSpec(memory_space=pl.ANY)
     near = pl.BlockSpec(memory_space=pltpu.VMEM)
     return pl.pallas_call(
         kernel,
@@ -567,25 +577,28 @@
             vmem((3, 80, CUT), bf16),
             vmem((3, 80, THIRD - CUT), bf16),
             vmem((3, 2, 80, THIRD), bf16),
-            vmem((3, 4, 32, THIRD), bf16),
-            vmem((3, 32, CUT), bf16),
-            vmem((3, 32, THIRD - CUT), bf16),
-            vmem((3, 2, 32, THIRD), bf16),
-            vmem((3, 4, 8, THIRD), full),
-            vmem((3, 3, 8, THIRD), full),
+            vmem((3, 4, 304, 128), bf16),
+            vmem((3, 3, 304, 128), bf16),
+            vmem((3, 4, 80, 128), bf16),
+            vmem((3, 3, 80, 128), bf16),
             vmem((1, PADDED), full),
             vmem((32, PADDED), F8),
             vmem((32, K), full),
             vmem((PADDED, K), F8),
             vmem((8, 1, K), full),
-            vmem((4, 1, K), full),
-            vmem((4, 1, K), full),
+            vmem((16, 1, K), full),
+            pltpu.SMEM((1,), jnp.int32),
+            pltpu.SMEM((1,), jnp.int32),
+            pltpu.SMEM((1,), jnp.int32),
+            pltpu.SMEM((1,), jnp.int32),
+            dma((4,)),
             dma((3,)),
             dma((8,)), dma((8,)),
             dma((2,)), dma((2,)),
             dma((3, 2, 4)), dma((3, 2, 4)),
             dma((3, 3)), dma((3, 3)),
-            dma((13,)), dma((13,)),
+            dma((3, 3)), dma((3, 3)),
+            dma((22,)), dma((22,)),
         ],
         compiler_params=pltpu.CompilerParams(
             collective_id=0, has_side_effects=True, vmem_limit_bytes=60 * 2**20

time: 88.8 us -> 79.7 us (0.90)
  Pallas kernels: 81.8 us -> 73.3 us
    pallas_call x1, Pallas kernels: 81.8 us -> 73.3 us  [call(): pl.pallas_call(kernel, out_shape=(jax.ShapeDtypeStruct(latent.shape, bf16...]
where the time goes in v4:
time: 79.7 us; the launch traced here: 79.5 us
  Pallas kernels  73.3 us (92%)
  between operations  3.22 us (4%)
  local copies, waits for them, and re-layouts  3 us (4%)
    pallas_call x1, Pallas kernels, call(): pl.pallas_call(kernel, out_shape=(jax.ShapeDtypeStruct(latent.shape, bf16...  73.3 us
    unnamed x2, local copies, waits for them, and re-layouts  3 us

profile of v4, /device:TPU:1, one launch (start us, length us, event | category | flops | bytes accessed | tf_op | source)
XLA Modules:
  0.0 79.5 jit_solution(11256905901019321154)
XLA Ops:
  3.2 73.3 %shard_map.95 = (bf16[1,8,32,640]{3,2,1,0:T(8,128)(2,1)}, f32[1,1024]{1,0:T(1,128)}) custom-call(s32[1]{0:T(128)S(6)} %copy.12.step_in, s32[1]{0:T(128)S(6)} %copy.13.noise_seed_in, s32[1]{0:T(128)S(6)} %copy.14.proj_seed_in, s32[1]{0:T(128)S(6)} %copy.15.example_in, bf16[1,8,32,640]{3,2,1,0:T(8,128)(2,1)} %latent_ref.1, bf16[640,640]{1,0:T(8,128)(2,1)} %time_ref.1, ...), custom_call_target="tpu_custom_call" | custom-call | tf_op jit(solution)/shard_map/pallas_call | solution.py:553
  76.5 1.7 %copy.16 = bf16[1,8,32,640]{3,2,1,0:T(8,128)(2,1)} copy(bf16[1,8,32,640]{3,2,1,0:T(8,128)(2,1)} %get-tuple-element.4) | data formatting | bytes 655360
  78.2 1.3 %copy.17 = f32[1,1024]{1,0:T(1,128)} copy(f32[1,1024]{1,0:T(1,128)} %get-tuple-element.5) | data formatting | bytes 8192

commit v5 on v4

--- a/solution.py
+++ b/solution.py
@@ -9,7 +9,7 @@
 from jax.sharding import PartitionSpec as P
 
 K = 1024
-FILLS = (8, 8, 0, 18, 34, 26)
+FILLS = (8, 12, 0, 20, 30, 22)
 M1 = 2146121005
 M2 = -2073254261
 MESH = pl.DeviceIdType.MESH
@@ -147,7 +147,8 @@
                 for half in range(2):
                     w = line + columns[half]
                     y = (w ^ shift_right(w, 15)) * jnp.int32(M2)
-                    rows = pl.ds(pl.multiple_of(step * 256 + part * 64 + half * 32, 32), 32)
+                    rows = step * 256 + part * 64 + half * 32
+                    rows = pl.ds(pl.multiple_of(rows, 32), 32)
                     bits[rows, j : j + 128] = lax.shift_right_arithmetic(y, 31).astype(jnp.int8).astype(F8)
         return carry
 
@@ -189,12 +190,13 @@
 
 
 def kernel(
-    step_in, noise_seed_in, proj_seed_in, example_in, latent_ref, time_ref, w1_ref, w2_ref,
-    section_ref, out_ref,
+    step_in, noise_seed_in, proj_seed_in, example_in, latent_in, time_in, w1_ref, w2_ref,
+    section_out, out_ref,
     stage, tall, side_in, corner_in, weight, actx, side_lhs, noise_keep, noisy_keep,
     hid_near, hid_far, cot_near, cot_far,
     lhs, s1, r1a, r1b, r1, s2, r2, s3, r3, row, grow, acc, bits,
     sum8, sum16, step_ref, noise_seed_ref, proj_seed_ref, example_ref, scalar_sem,
+    latent_ref, time_ref, section_ref, whole_sem,
     load_sem, rim_send, rim_recv,
     pair_send, pair_recv, ring_send, ring_recv, two_send, two_recv, tail_send, tail_recv, all_send, all_recv,
 ):
@@ -220,6 +222,8 @@
         rows = pl.ds(part * THIRD, THIRD)
         return pltpu.make_async_copy(source.at[rows], weight.at[rows], load_sem.at[part])
 
+    latent_copy = pltpu.make_async_copy(latent_in, latent_ref, whole_sem.at[0])
+    latent_copy.start()
     scalars = []
     for index, (source, held) in enumerate((
         (step_in, step_ref), (noise_seed_in, noise_seed_ref),
@@ -229,6 +233,8 @@
         scalars[-1].start()
     for part in range(3):
         load(w1_ref, part).start()
+    time_copy = pltpu.make_async_copy(time_in, time_ref, whole_sem.at[1])
+    time_copy.start()
     for copy in scalars:
         copy.wait()
 
@@ -249,6 +255,7 @@
             rows.append(jnp.zeros((16 - len(rows), CH), jnp.float32))
         return rounded(jnp.concatenate(rows, axis=0))
 
+    latent_copy.wait()
     edge = {-1: (0, 1), 1: (TW - 2, TW - 1)}
     brim = {-1: (0, 1), 1: (TH - 2, TH - 1)}
     for index, dc in enumerate((-1, 1)):
@@ -315,6 +322,7 @@
     angle = when * jnp.exp(f32(half) * (-math.log(10000.0)) / (CH // 2))
     wave = jnp.where(lane < CH // 2, jnp.sin(angle), jnp.cos(angle))
     wave = rounded(jnp.concatenate([wave, jnp.zeros((15, CH), jnp.float32)], axis=0))
+    time_copy.wait()
     temb = jnp.dot(wave, time_ref[...], preferred_element_type=jnp.float32)[0:1]
     fill(FILLS[1])
     for copy in rims:
@@ -409,6 +417,8 @@
         full = f32(noisy_keep[r]) + total[r * TW : (r + 1) * TW]
         section_ref[0, r] = rounded(full)
         cot_near[r * TW : (r + 1) * TW] = rounded((full - noise_keep[r]) * (1.0 / math.sqrt(ROWS * COLS)))
+    section_copy = pltpu.make_async_copy(section_ref, section_out, whole_sem.at[2])
+    section_copy.start()
     pair.append(send(cot_near, cot_far, pair_send.at[0], pair_recv.at[0], partner))
     started += pair
     picks = [selection(third, at["core"]) for third in range(3)]
@@ -540,6 +550,7 @@
         for index in range(1, count + 1):
             share = share + slots[index]
     out_ref[...] = share
+    section_copy.wait()
     for copy in started:
         copy.wait_send()
 
@@ -548,16 +559,15 @@
     bf16, full = jnp.bfloat16, jnp.float32
     vmem = pltpu.VMEM
     dma = pltpu.SemaphoreType.DMA
-    scalar = pl.BlockSpec(memory_space=pl.ANY)
-    near = pl.BlockSpec(memory_space=pltpu.VMEM)
+    far = pl.BlockSpec(memory_space=pl.ANY)
     return pl.pallas_call(
         kernel,
         out_shape=(
             jax.ShapeDtypeStruct(latent.shape, bf16),
             jax.ShapeDtypeStruct((1, K), full),
         ),
-        in_specs=[scalar] * 4 + [near] * 2 + [pl.BlockSpec(memory_space=pl.ANY)] * 2,
-        out_specs=(near, near),
+        in_specs=[far] * 8,
+        out_specs=(far, pl.BlockSpec(memory_space=pltpu.VMEM)),
         scratch_shapes=[
             vmem((6, 16, CH), bf16),
             vmem((2, 2, TW, CH), bf16),
@@ -592,6 +602,10 @@
             pltpu.SMEM((1,), jnp.int32),
             pltpu.SMEM((1,), jnp.int32),
             dma((4,)),
+            vmem(latent.shape, bf16),
+            vmem(time_weight.shape, bf16),
+            vmem(latent.shape, bf16),
+            dma((3,)),
             dma((3,)),
             dma((8,)), dma((8,)),
             dma((2,)), dma((2,)),

time: 79.7 us -> 78.3 us (0.982)
  Pallas kernels: 73.3 us -> 71.9 us
    pallas_call x1, Pallas kernels: 73.3 us -> 71.9 us  [call(): pl.pallas_call(kernel, out_shape=(jax.ShapeDtypeStruct(latent.shape, bf16...]
where the time goes in v5:
time: 78.3 us; the launch traced here: 78.1 us
  Pallas kernels  71.9 us (92%)
  between operations  3.22 us (4%)
  local copies, waits for them, and re-layouts  3 us (4%)
    pallas_call x1, Pallas kernels, call(): pl.pallas_call(kernel, out_shape=(jax.ShapeDtypeStruct(latent.shape, bf16...  71.9 us
    unnamed x2, local copies, waits for them, and re-layouts  3 us

profile of v5, /device:TPU:1, one launch (start us, length us, event | category | flops | bytes accessed | tf_op | source)
XLA Modules:
  0.0 78.1 jit_solution(3143802471532880113)
XLA Ops:
  3.2 71.9 %shard_map.95 = (bf16[1,8,32,640]{3,2,1,0:T(8,128)(2,1)}, f32[1,1024]{1,0:T(1,128)}) custom-call(s32[1]{0:T(128)S(6)} %copy.12.step_in, s32[1]{0:T(128)S(6)} %copy.13.noise_seed_in, s32[1]{0:T(128)S(6)} %copy.14.proj_seed_in, s32[1]{0:T(128)S(6)} %copy.15.example_in, bf16[1,8,32,640]{3,2,1,0:T(8,128)(2,1)} %latent_in.1, bf16[640,640]{1,0:T(8,128)(2,1)} %time_in.1, ...), custom_call_target="tpu_custom_call" | custom-call | tf_op jit(solution)/shard_map/pallas_call | solution.py:563
  75.1 1.7 %copy.16 = bf16[1,8,32,640]{3,2,1,0:T(8,128)(2,1)} copy(bf16[1,8,32,640]{3,2,1,0:T(8,128)(2,1)} %get-tuple-element.4) | data formatting | bytes 655360
  76.8 1.3 %copy.17 = f32[1,1024]{1,0:T(1,128)} copy(f32[1,1024]{1,0:T(1,128)} %get-tuple-element.5) | data formatting | bytes 8192

commit v6 on v5

--- a/solution.py
+++ b/solution.py
@@ -446,6 +446,12 @@
                  ring_send.at[third, level, 0], ring_recv.at[third, level, 0], up),
             send(blocks.at[third, across, :, pl.ds(CUT, THIRD - CUT)], rb.at[third],
                  ring_send.at[third, level, 1], ring_recv.at[third, level, 1], down),
+            send(blocks.at[third, hop(at, axis, 1), :, pl.ds(CUT, THIRD - CUT)],
+                 r1.at[third, 0, :, pl.ds(CUT, THIRD - CUT)],
+                 ring_send.at[third, level, 4], ring_recv.at[third, level, 4], up),
+            send(blocks.at[third, hop(at, axis, -1), :, pl.ds(0, CUT)],
+                 r1.at[third, 1, :, pl.ds(0, CUT)],
+                 ring_send.at[third, level, 5], ring_recv.at[third, level, 5], down),
         ]
 
     def ring_two(third, level, blocks, ra, rb, first, landed):
@@ -455,13 +461,13 @@
         first[0].wait_recv()
         old = blocks[third, above, :, 0:CUT]
         blocks[third, above, :, 0:CUT] = (f32(old) + f32(ra[third])).astype(jnp.bfloat16)
-        up = send(blocks.at[third, above], landed.at[third, 0],
+        up = send(blocks.at[third, above, :, pl.ds(0, CUT)], landed.at[third, 0, :, pl.ds(0, CUT)],
                   ring_send.at[third, level, 2], ring_recv.at[third, level, 2],
                   device(at, **{axis: above}))
         first[1].wait_recv()
         old = blocks[third, below, :, CUT:THIRD]
         blocks[third, below, :, CUT:THIRD] = (f32(old) + f32(rb[third])).astype(jnp.bfloat16)
-        down = send(blocks.at[third, below], landed.at[third, 1],
+        down = send(blocks.at[third, below, :, pl.ds(CUT, THIRD - CUT)], landed.at[third, 1, :, pl.ds(CUT, THIRD - CUT)],
                     ring_send.at[third, level, 3], ring_recv.at[third, level, 3],
                     device(at, **{axis: below}))
         return [up, down]
@@ -500,7 +506,7 @@
     seconds = []
     for third in range(3):
         mine = at[ORDERS[third][0]]
-        for copy in twos[third]:
+        for copy in twos[third] + ones[third][2:]:
             copy.wait_recv()
         total = f32(s1[third, mine]) + f32(r1[third, 0]) + f32(r1[third, 1])
         for block in range(4):
@@ -609,7 +615,7 @@
             dma((3,)),
             dma((8,)), dma((8,)),
             dma((2,)), dma((2,)),
-            dma((3, 2, 4)), dma((3, 2, 4)),
+            dma((3, 2, 6)), dma((3, 2, 6)),
             dma((3, 3)), dma((3, 3)),
             dma((3, 3)), dma((3, 3)),
             dma((22,)), dma((22,)),

time: 78.3 us -> 77.7 us (level)
  no operation moved by 1% of the time
where the time goes in v6:
time: 77.7 us; the launch traced here: 77.5 us
  Pallas kernels  71.3 us (92%)
  between operations  3.22 us (4%)
  local copies, waits for them, and re-layouts  3 us (4%)
    pallas_call x1, Pallas kernels, call(): pl.pallas_call(kernel, out_shape=(jax.ShapeDtypeStruct(latent.shape, bf16...  71.3 us
    unnamed x2, local copies, waits for them, and re-layouts  3 us

profile of v6, /device:TPU:1, one launch (start us, length us, event | category | flops | bytes accessed | tf_op | source)
XLA Modules:
  0.0 77.5 jit_solution(3692137723578739989)
XLA Ops:
  3.2 71.3 %shard_map.95 = (bf16[1,8,32,640]{3,2,1,0:T(8,128)(2,1)}, f32[1,1024]{1,0:T(1,128)}) custom-call(s32[1]{0:T(128)S(6)} %copy.12.step_in, s32[1]{0:T(128)S(6)} %copy.13.noise_seed_in, s32[1]{0:T(128)S(6)} %copy.14.proj_seed_in, s32[1]{0:T(128)S(6)} %copy.15.example_in, bf16[1,8,32,640]{3,2,1,0:T(8,128)(2,1)} %latent_in.1, bf16[640,640]{1,0:T(8,128)(2,1)} %time_in.1, ...), custom_call_target="tpu_custom_call" | custom-call | tf_op jit(solution)/shard_map/pallas_call | solution.py:569
  74.5 1.7 %copy.16 = bf16[1,8,32,640]{3,2,1,0:T(8,128)(2,1)} copy(bf16[1,8,32,640]{3,2,1,0:T(8,128)(2,1)} %get-tuple-element.4) | data formatting | bytes 655360
  76.2 1.3 %copy.17 = f32[1,1024]{1,0:T(1,128)} copy(f32[1,1024]{1,0:T(1,128)} %get-tuple-element.5) | data formatting | bytes 8192
